TPU v7x, 32 devices: a whole 2x2x4 slice. The times are simulated.
32 devices in a mesh: chain: 8 (over z, y), sub: 4 (over x, core).
Axes of the slice: x: 2, y: 2, z: 4, core: 2. Of those that a mesh axis runs over, the one named last changes fastest.
Arguments:
- rhs: float32 [192, 5, 8, 512], P('chain', None, None, 'sub'), may hold values from -100 to 100
- diag_block: float32 [192, 5, 5, 512], P('chain', None, None, 'sub')
- diag_inverse: float32 [192, 5, 5, 512], P('chain', None, None, 'sub'), as said below
- lower_coef: float32 [192, 2, 5, 5, 512], P('chain', None, None, None, 'sub')
- upper_coef: float32 [192, 2, 5, 5, 512], P('chain', None, None, None, 'sub')
- side_coef: float32 [192, 2, 5, 5, 512], P('chain', None, None, None, 'sub')
- lower_cols: int32 [192, 2], P('chain'), may hold values from -3 to 190, as said below
- upper_cols: int32 [192, 2], P('chain'), may hold values from 1 to 194, as said below
- counts: int32 [192, 2], P('chain'), may hold values from 1 to 2
Outputs:
- correction: float32 [192, 5, 8, 512], P('chain', None, None, 'sub')
- residual_unit: float32 [192, 5, 8, 512], P('chain', None, None, 'sub')
Inputs may be any that keep to these rules, and one draw needn't show every extreme that they name: lower_cols[b, k] = b - d with d from 1 to 3, the two slots of a block differ, and some block has d = 3. upper_cols[b, k] = b + d with d from 1 to 3, the two slots of a block differ, and some block has d = 3. diag_inverse is the inverse of diag_block at every block and cell.
All inputs are finite; a program needn't handle non-finite values.
Results may differ from a plain program's by a relative error of at most 0.0003.
Values sent between devices are 32-bit elements; how exact they have to be, the bound alone decides.
No kernel may reach another device: no remote copies, remote signals or barrier semaphores. Data moves between devices by JAX's collectives and lax.ppermute only.
A program may use at most 128 MiB of HBM per device.

v0:
```python
import functools

import jax
import jax.numpy as jnp
from jax import lax
from jax.experimental import pallas as pl
from jax.experimental.pallas import tpu as pltpu
from jax.sharding import PartitionSpec as P

VARS = 5
REACH = 3
SLOTS = 2
STATE = REACH * VARS
WIDE = 16
PAD = 8
SPACE = 72
DIRECT = 4
VMEM_LIMIT = 40 * 1024 * 1024

VMEM = pltpu.VMEM
SMEM = pltpu.SMEM
HBM = pltpu.HBM


def lanes_of(cells):
    return lax.broadcasted_iota(jnp.int32, (8, cells), 1)


def block_transpose(items, width, cells):
    count = len(items)
    lane = lanes_of(cells)
    half = 1
    while half < count:
        bit = (lane // (half * width)) % 2 == 1
        out = list(items)
        for a in range(count):
            if a & half:
                continue
            b = a + half
            out[a] = jnp.where(bit, pltpu.roll(items[b], half * width, 1), items[a])
            out[b] = jnp.where(bit, items[b], pltpu.roll(items[a], cells - half * width, 1))
        items = out
        half *= 2
    return items


def spread(ref, place, row):
    return ref[place + (pl.ds(row, 8, stride=0), slice(None))]


def mul_rows(rows, near):
    total = rows[0] * near[0]
    for j in range(1, len(near)):
        total = total + rows[j] * near[j]
    return total


def mul_groups(rows, nears):
    return [mul_rows(rows, [near[g] for near in nears]) for g in range(len(nears[0]))]


def couple(mats, b, nears):
    out = []
    for i in range(VARS):
        parts = [
            mul_groups([spread(mats, (i, j, k), b) for j in range(VARS)], nears[k])
            for k in range(SLOTS)
        ]
        out.append([x + y for x, y in zip(*parts)])
    return out


def apply_coef(coef, b, nears):
    out = []
    for i in range(VARS):
        parts = []
        for k in range(SLOTS):
            place = (b * VARS + i) * VARS * SLOTS + k
            parts.append(
                mul_rows([spread(coef, (), place + SLOTS * j) for j in range(VARS)], nears[k])
            )
        out.append(parts[0] + parts[1])
    return out


def products(inv, coef, out):
    blocks = out.shape[3] - PAD
    stride = VARS * VARS * SLOTS

    def some(o, carry):
        start = o * 8
        left = [[-inv[i, m, pl.ds(start, 8), :] for m in range(VARS)] for i in range(VARS)]
        for k in range(SLOTS):
            stores = []
            for j in range(VARS):
                place = start * stride + j * SLOTS + k
                right = [
                    coef[pl.ds(place + m * VARS * SLOTS, 8, stride=stride), :] for m in range(VARS)
                ]
                for i in range(VARS):
                    here = (i, j, k, pl.ds(start, 8))
                    stores.append((out, here, mul_rows(left[i], right)))
            store_all(stores)
        return carry

    steps(blocks // 8, 3, some)


def slots(cols, counts, side, b, shift, empty):
    return [jnp.where(k < counts[side, b], cols[k, b] + shift, empty) for k in range(SLOTS)]


def read_block(buf, place):
    return [buf[place, v] for v in range(VARS)]


def read_groups(buf, place):
    count = buf.shape[2] // 8
    return [[buf[place, v, pl.ds(8 * g, 8), :] for g in range(count)] for v in range(VARS)]


class Kept:
    def __init__(self, carry, stores):
        self.carry, self.stores = carry, stores


def store_all(stores):
    for ref, place, value in stores:
        ref[place] = value


def steps(count, most, body, carry=0):
    unroll = max(u for u in range(1, most + 1) if count % u == 0)

    def chunk(o, carry):
        kept = []
        for u in range(unroll):
            carry = body(o * unroll + u, carry)
            if isinstance(carry, Kept):
                kept += carry.stores
                carry = carry.carry
        store_all(kept)
        return carry

    return lax.fori_loop(0, count // unroll, chunk, carry)


def column_order(nrhs):
    wide_y = nrhs + WIDE
    order = []
    for first, count in ((nrhs, STATE), (wide_y + nrhs, STATE - 1), (wide_y + nrhs + WIDE, STATE)):
        order += [(half, first + j) for half in range(2) for j in range(count)]
    for first in (0, wide_y):
        order += [(half, first + q) for half in range(2) for q in range(nrhs)]
    return order


def position(n):
    return lax.axis_index("chain") % n


def gather_parts(parts, buf):
    here = position(buf.shape[0])
    for x, part in enumerate(parts):
        for page in range(part.shape[0]):
            buf[here ^ x, page] = part[page]


def scatter_parts(buf, parts):
    here = position(buf.shape[0])
    for x, part in enumerate(parts):
        for page in range(part.shape[0]):
            part[page] = buf[here ^ x, page]


def parted(kernel, before, count, n, *refs):
    if count == 1:
        return kernel(*refs)
    outs, buf = refs[before : before + count], refs[-1]
    kernel(*refs[:before], buf, *refs[before + count : -1])
    scatter_parts(buf, outs)


def joined(kernel, count, n, *refs):
    if count == 1:
        return kernel(*refs)
    gather_parts(refs[:count], refs[-1])
    kernel(refs[-1], *refs[count:-1])


def exchange(parts, n, groups):
    if len(parts) == 1:
        return [lax.all_to_all(parts[0], "chain", 0, 0, tiled=True, axis_index_groups=groups)]
    count = lax.axis_size("chain")
    parts = list(parts)
    for x in [len(parts) - 1] + list(range(1, len(parts) - 1)):
        parts[x] = lax.ppermute(parts[x], "chain", [(i, i ^ x) for i in range(count)])
    return parts


def local_kernel(
    n,
    rhs_h,
    inv_h,
    low_h,
    upp_h,
    lcols_h,
    ucols_h,
    counts_h,
    out,
    source,
    mlow,
    mupp,
    lcols_v,
    ucols_v,
    counts_v,
    rhs,
    inv,
    low,
    upp,
    lcols,
    ucols,
    counts,
    ybuf,
    zbuf,
    stage,
    sems,
):
    copies = [
        pltpu.make_async_copy(src, dst, sems.at[k])
        for k, (src, dst) in enumerate(
            (
                (inv_h, inv.at[:, :, pl.ds(0, rhs.shape[0]), :]),
                (low_h, low),
                (lcols_h, lcols),
                (counts_h, counts),
                (ucols_h, ucols),
                (rhs_h, rhs),
                (upp_h, upp),
                (lcols_h, lcols_v),
                (ucols_h, ucols_v),
                (counts_h, counts_v),
            )
        )
    ]
    for copy in copies:
        copy.start()
    blocks, _, nrhs, cells = rhs.shape
    base = lax.axis_index("chain") * blocks
    wide_y = nrhs + WIDE
    wide_z = wide_y + WIDE
    row_y = lax.broadcasted_iota(jnp.int32, (wide_y, cells), 0)
    row_z = lax.broadcasted_iota(jnp.int32, (wide_z, cells), 0)
    for m in range(REACH):
        for v in range(VARS):
            q = VARS * m + v
            ybuf[REACH - 1 - m, v] = (row_y == nrhs + q).astype(jnp.float32)
            zbuf[blocks + m, v] = (row_z == wide_y + q).astype(jnp.float32)
    for v in range(VARS):
        ybuf[blocks + REACH, v] = jnp.zeros((wide_y, cells), jnp.float32)
        zbuf[blocks + REACH, v] = jnp.zeros((wide_z, cells), jnp.float32)
    empty = blocks + REACH
    copies[0].wait()
    copies[1].wait()
    products(inv, low, mlow)
    for copy in copies[2:6]:
        copy.wait()

    def first(b, carry):
        nears = [read_groups(ybuf, s) for s in slots(lcols, counts, 0, b, REACH - base, empty)]
        acc = couple(mlow, b, nears)
        right = [rhs[b, i] for i in range(VARS)]
        stores = []
        for i in range(VARS):
            own = mul_rows([spread(inv, (i, j), b) for j in range(VARS)], right)
            stores.append((source, (b, i), own))
            for g in range(len(acc[i])):
                value = own + acc[i][0] if g == 0 else acc[i][g]
                stores.append((ybuf, (b + REACH, i, pl.ds(8 * g, 8)), value))
        store_all(stores)
        return carry

    steps(blocks, 6, first)
    for copy in copies[6:]:
        copy.wait()
    products(inv, upp, mupp)

    def second(e, carry):
        c = blocks - 1 - e
        nears = [read_groups(zbuf, s) for s in slots(ucols, counts, 1, c, -base, empty)]
        acc = couple(mupp, c, nears)
        stores = []
        for i in range(VARS):
            for g in range(len(acc[i])):
                if g < wide_y // 8:
                    value = ybuf[c + REACH, i, 8 * g : 8 * g + 8] + acc[i][g]
                else:
                    value = acc[i][g]
                stores.append((zbuf, (c, i, pl.ds(8 * g, 8)), value))
        store_all(stores)
        return carry

    steps(blocks, 6, second)

    zero = jnp.zeros((8, cells), jnp.float32)
    for i in range(WIDE):
        m, v = i // VARS, i % VARS
        for g in range((wide_y + wide_z) // 8):
            if i == STATE:
                value = zero
            elif g < wide_y // 8:
                value = ybuf[blocks + REACH - 1 - m, v, 8 * g : 8 * g + 8]
            else:
                value = zbuf[m, v, 8 * g - wide_y : 8 * g - wide_y + 8]
            stage[pl.ds(i * SPACE + 8 * g, 8), :] = value

    def column(half, index):
        return stage[pl.ds(half * 8 * SPACE + index, 8, stride=SPACE), :]

    for half in range(2):
        place = STATE * SPACE + nrhs + 8 * half
        stage[pl.ds(place, 8), :] = column(half, wide_y + nrhs + STATE - 1)
    order = column_order(nrhs)
    width = cells // n
    for page in range(out.shape[1]):
        items = [column(*at) for at in order[page * n : (page + 1) * n]]
        items += [zero] * (n - len(items))
        for k, item in enumerate(block_transpose(items, width, cells)):
            out[k, page] = item


def split(value, period, stop, width, cells):
    items = [value]
    lane = lanes_of(cells)
    while period > stop:
        half = period // 2 * width
        bit = lane // half % 2 == 1
        fresh = []
        for item in items:
            other = pltpu.roll(item, half, 1)
            fresh += [jnp.where(bit, other, item), jnp.where(bit, item, other)]
        items = fresh
        period //= 2
    return items


def total_of(terms):
    while len(terms) > 1:
        pairs = [terms[k] + terms[k + 1] for k in range(0, len(terms) - 1, 2)]
        terms = pairs + terms[len(terms) - len(terms) % 2 :]
    return terms[0]


COLUMNS = 6 * STATE - 2


def store_state(buf, state):
    for half in range(2):
        for g, value in enumerate(state[half]):
            buf[pl.ds(g * WIDE + 8 * half, 8), :] = value


def state_rows(buf, count):
    return [[spread(buf, (), g * WIDE + j) for j in range(STATE)] for g in range(count)]


def pass_forward(d, cols, sides, state, buf, keep):
    groups, extra = len(state[0]), sides.shape[1] // 4
    store_state(buf, state)
    rows = state_rows(buf, groups)
    fresh = []
    for half in range(2):
        columns = [cols[pl.ds((d * COLUMNS + half * STATE + j) * 8, 8), :] for j in range(STATE)]
        fresh.append([])
        for g in range(groups):
            total = total_of([c * r for c, r in zip(columns, rows[g])])
            fresh[half].append(total + sides[d, half * extra + g] if g < extra else total)
        first = d * COLUMNS + 2 * STATE + half * (STATE - 1)
        columns = [cols[pl.ds((first + j) * 8, 8), :] for j in range(STATE - 1)]
        start = (d * COLUMNS + STATE + 8 * half) * 8 + 7
        columns.append(cols[pl.ds(start, 8, stride=8), :])
        for g in range(groups):
            total = total_of([c * r for c, r in zip(columns, rows[g])])
            if g < extra:
                total = total + sides[d, (2 + half) * extra + g]
            keep[d, half * groups + g] = total
    return fresh


def pass_back(d, cols, state, buf, keep):
    groups = len(state[0])
    store_state(buf, state)
    rows = state_rows(buf, groups)
    fresh = []
    for half in range(2):
        first = d * COLUMNS + 4 * STATE - 2 + half * STATE
        columns = [cols[pl.ds((first + j) * 8, 8), :] for j in range(STATE)]
        fresh.append(
            [
                total_of([c * r for c, r in zip(columns, rows[g])]) + keep[d, half * groups + g]
                for g in range(groups)
            ]
        )
    return fresh


def flat(state):
    return tuple(state[0] + state[1])


def folded(values):
    groups = len(values) // 2
    return [list(values[:groups]), list(values[groups:])]


def first_solve_kernel(x, cols, sides, offer, keep, buf):
    n, cells = x.shape[0], x.shape[3]
    width = cells // n
    packed = min(8, n)
    extra, groups = sides.shape[1] // 4, offer.shape[0] // 2
    zero = jnp.zeros((8, cells), jnp.float32)

    def unpack(d, carry):
        values = [x[d, page] for page in range(x.shape[1])]
        for page, value in enumerate(values):
            for k, block in enumerate(split(value, n, packed, width, cells)):
                e = page * n + k * packed
                if e < COLUMNS:
                    for g, item in enumerate(split(block, packed, 1, width, cells)):
                        cols[pl.ds((d * COLUMNS + e + g) * 8, 8), :] = item
                elif e < COLUMNS + 4 * 8:
                    sides[d, (e - COLUMNS) // packed] = block
        return carry

    steps(n, 2, unpack)
    lane = lanes_of(cells)
    row = lax.broadcasted_iota(jnp.int32, (8, cells), 0)
    start = []
    for half in range(2):
        start.append([zero] * extra)
        for g in range(groups - extra):
            column = lane // width % packed + g * packed
            start[half].append((column == row + 8 * half).astype(jnp.float32))

    def ahead(d, state):
        return flat(pass_forward(d, cols, sides, folded(state), buf, keep))

    leaving = steps(n, 2, ahead, flat(start))

    def back(e, state):
        return flat(pass_back(n - 1 - e, cols, folded(state), buf, keep))

    left = steps(n, 2, back, (zero,) * (2 * groups))
    is_left = lax.axis_index("chain") < n
    for e in range(2 * groups):
        offer[e] = jnp.where(is_left, leaving[e], left[e])


def second_solve_kernel(cols, sides, mine, got, out, keep, buf, states):
    n, cells = out.shape[0], out.shape[3]
    width = cells // n
    packed = min(8, n)
    extra, groups = sides.shape[1] // 4, mine.shape[0] // 2
    zero = jnp.zeros((8, cells), jnp.float32)
    is_left = lax.axis_index("chain") < n
    store_state(buf, [[mine[half * groups + g] for g in range(extra)] for half in range(2)])
    rows = state_rows(buf, extra)
    entering, far = [], []
    for half in range(2):
        columns = []
        for g in range(extra, groups):
            columns += split(got[half * groups + g], packed, 1, width, cells)
        for g in range(extra):
            known = got[half * groups + g]
            total = total_of([c * r for c, r in zip(columns, rows[g])])
            entering.append(jnp.where(is_left, 0.0, known))
            far.append(jnp.where(is_left, known + total, 0.0))

    def ahead(d, state):
        for e in range(2 * extra):
            states[d, e] = state[e]
        return flat(pass_forward(d, cols, sides, folded(state), buf, keep))

    steps(n, 4, ahead, tuple(entering))

    def back(e, state):
        d = n - 1 - e
        for e in range(2 * extra):
            states[d, 2 * extra + e] = state[e]
        return flat(pass_back(d, cols, folded(state), buf, keep))

    steps(n, 4, back, tuple(far))
    block = lanes_of(cells) // (packed * width)

    def pack(d, carry):
        for page in range(out.shape[1]):
            total = zero
            for r in range(4 * extra):
                if packed * r // n == page:
                    total = jnp.where(block == packed * r % n // packed, states[d, r], total)
            out[d, page] = total
        return carry

    steps(n, 4, pack)


def sweep_kernel(
    n,
    states,
    source,
    mlow,
    mupp,
    lcols,
    ucols,
    counts,
    low_h,
    side_h,
    zout,
    wout,
    tail,
    edge,
    low,
    side,
    ybuf,
    stage,
    sems,
):
    total = low_h.shape[0]
    copies = [
        pltpu.make_async_copy(src, dst.at[pl.ds(0, total), :], sems.at[k])
        for k, (src, dst) in enumerate(((low_h, low), (side_h, side)))
    ]
    for copy in copies:
        copy.start()
    blocks, _, nrhs, cells = source.shape
    base = lax.axis_index("chain") * blocks
    width = cells // n
    zero = jnp.zeros((nrhs, cells), jnp.float32)
    items = []
    for r in range(states.shape[1]):
        items += block_transpose([states[k, r] for k in range(n)], width, cells)
    for e in range(32):
        stage[pl.ds(8 * e, 8), :] = items[e]

    def entering(start):
        rows = [stage[pl.ds(start + q // 8 * 64 + q % 8, 8, stride=8), :] for q in range(STATE)]
        return tuple(rows)

    lane = lanes_of(cells)
    for v in range(VARS):
        wout[blocks, v] = zero

    def near(window, b, sign, cols, side):
        nears = []
        for k in range(SLOTS):
            off = sign * (cols[k, b] - base - b)
            picks = []
            for v in range(VARS):
                value = window[(REACH - 1) * VARS + v]
                for d in range(REACH - 1):
                    value = jnp.where(off == d + 1, window[d * VARS + v], value)
                picks.append(value if k == 0 else jnp.where(k < counts[side, b], value, 0.0))
            nears.append([[value] for value in picks])
        return nears

    def first(b, window):
        acc = couple(mlow, b, near(window, b, -1, lcols, 0))
        fresh = tuple(source[b, i] + acc[i][0] for i in range(VARS))
        return Kept(fresh + window[: STATE - VARS], [(ybuf, (b, i), fresh[i]) for i in range(VARS)])

    steps(blocks, 8, first, entering(0))

    def second(e, carry):
        c = blocks - 1 - e
        window, edges = carry[:STATE], list(carry[STATE:])
        acc = couple(mupp, c, near(window, c, 1, ucols, 1))
        fresh = tuple(ybuf[c, i] + acc[i][0] for i in range(VARS))
        here = (lane == 2 * c) | (lane == (2 * c + cells - 1) % cells)
        stores = []
        for i in range(VARS):
            stores += [(zout, (c, i), fresh[i]), (wout, (c, i), acc[i][0])]
            edges[i] = jnp.where(here, pltpu.roll(fresh[i], 2 * c, 1), edges[i])
        return Kept(fresh + window[: STATE - VARS] + tuple(edges), stores)

    carry = steps(blocks, 8, second, entering(128) + (zero,) * VARS)
    for v in range(VARS):
        edge[v] = carry[STATE + v]
    for m in range(REACH):
        for v in range(VARS):
            tail[m, v] = wout[blocks - REACH + m, v]
    for copy in copies:
        copy.wait()


def inner_kernel(z, w, low, side, lcols, counts, resid, coef, correction, wbuf, sem):
    store = pltpu.make_async_copy(z, correction, sem)
    store.start()
    blocks, _, nrhs, cells = z.shape
    base = lax.axis_index("chain") * blocks
    lane = lanes_of(cells)
    zero = jnp.zeros((nrhs, cells), jnp.float32)
    for v in range(VARS):
        for m in range(REACH):
            wbuf[m, v] = zero
            wbuf[m + REACH, v] = w[m, v]
        wbuf[2 * REACH, v] = zero
    pages = coef.shape[0]
    size = VARS * VARS * SLOTS
    row = lax.broadcasted_iota(jnp.int32, (8, cells), 0)

    def block(b, found, buf, shift, empty):
        nears = [read_block(buf, s) for s in slots(lcols, counts, 0, b, shift - base, empty)]
        acc = apply_coef(low, b, nears)
        left, right = [], []
        for v in range(VARS):
            here = z[b, v]
            left.append(jnp.where(lane == 0, 0.0, pltpu.roll(here, 1, 1)))
            right.append(jnp.where(lane == cells - 1, 0.0, pltpu.roll(here, cells - 1, 1)))
        beside = apply_coef(side, b, [left, right])
        here = (lane + row % 2) % cells == 2 * b
        found = tuple(
            jnp.where(here, pltpu.roll(side[pl.ds(b * size + 8 * r, 8), :], 2 * b, 1), found[r])
            for r in range(pages)
        )
        return Kept(found, [(resid, (b, i), acc[i] + beside[i]) for i in range(VARS)])

    found = (jnp.zeros((8, cells), jnp.float32),) * pages
    for b in range(REACH):
        kept = block(b, found, wbuf, REACH, 2 * REACH)
        store_all(kept.stores)
        found = kept.carry

    def inner(b, found):
        return block(b + REACH, found, w, 0, blocks)

    found = steps(blocks - REACH, 7, inner, found)
    for r in range(pages):
        coef[r] = found[r]
    store.wait()


def outer_kernel(
    inner, coef, low, tail, swap_a, swap_b, lcols, counts, resid, squares, wbuf
):
    blocks, _, nrhs, cells = inner.shape
    base = lax.axis_index("chain") * blocks
    first_block = lax.axis_index("chain") == 0
    place = lax.axis_index("sub")
    odd = place % 2 == 1
    first, last = place == 0, place == lax.axis_size("sub") - 1
    lane = lanes_of(cells)
    zero = jnp.zeros((nrhs, cells), jnp.float32)
    near = []
    for v in range(VARS):
        west = jnp.where(first, 0.0, jnp.where(odd, swap_a[v], swap_b[v]))
        east = jnp.where(last, 0.0, jnp.where(odd, swap_b[v], swap_a[v]))
        west, east = pltpu.roll(west, 1, 1), pltpu.roll(east, cells - 1, 1)
        near.append(jnp.where(lane % 2 == 0, west, east))
    edge = []
    for i in range(VARS):
        rows = []
        for j in range(VARS):
            k = (i * VARS + j) * SLOTS
            rows.append(coef[k // 8, pl.ds(k % 8, 1), :] + coef[(k + 1) // 8, pl.ds((k + 1) % 8, 1), :])
        edge.append(mul_rows(rows, near))
    for v in range(VARS):
        for m in range(REACH):
            wbuf[m, v] = jnp.where(first_block, 0.0, tail[m, v])
        wbuf[REACH, v] = zero
    ends = (lane == 0) | (lane == cells - 1)

    def add(b, values, totals):
        stores, fresh = [], []
        for i in range(VARS):
            other = pltpu.roll(edge[i], (cells - 2 * b) % cells, 1)
            value = values[i] + jnp.where(ends, other, 0.0)
            stores.append((resid, (b, i), value))
            fresh.append(totals[i] + value * value)
        return Kept(tuple(fresh), stores)

    totals = (zero,) * VARS
    stores = []
    for b in range(REACH):
        places = [
            jnp.where(s < REACH, s, REACH) for s in slots(lcols, counts, 0, b, REACH - base, REACH)
        ]
        acc = apply_coef(low, b, [read_block(wbuf, s) for s in places])
        kept = add(b, [inner[b, i] + acc[i] for i in range(VARS)], totals)
        stores += kept.stores
        totals = kept.carry
    store_all(stores)

    def rest(b, totals):
        return add(b + REACH, [inner[b + REACH, i] for i in range(VARS)], totals)

    totals = steps(blocks - REACH, 7, rest, totals)
    total = totals[0]
    for i in range(1, VARS):
        total = total + totals[i]
    sums = jnp.broadcast_to(jnp.sum(total, axis=1, keepdims=True), total.shape)
    row = lax.broadcasted_iota(jnp.int32, total.shape, 0)
    line = jnp.sum(jnp.where(lane == row, sums, 0.0), axis=0, keepdims=True)
    for p in range(squares.shape[0]):
        squares[p] = line


def scale_kernel(entries, resid, squares, out, scaled, sems):
    blocks, _, nrhs, cells = resid.shape
    line = squares[0]
    for p in range(1, squares.shape[0]):
        line = line + squares[p]
    lane = lanes_of(cells)
    row = lax.broadcasted_iota(jnp.int32, (nrhs, cells), 0)
    line = jnp.where(lane == row, jnp.broadcast_to(line, (nrhs, cells)), 0.0)
    msq = jnp.sum(line, axis=1, keepdims=True) / entries
    factor = jnp.broadcast_to(-lax.rsqrt(msq + 1e-06), (nrhs, cells))

    count = sems.shape[0]
    size = blocks // count
    copies = []
    for part in range(count):
        stores = [
            (scaled, (b, v), resid[b, v] * factor)
            for b in range(part * size, (part + 1) * size)
            for v in range(VARS)
        ]
        store_all(stores)
        here = pl.ds(part * size, size)
        copies.append(pltpu.make_async_copy(scaled.at[here], out.at[here], sems.at[part]))
        copies[part].start()
    for copy in copies:
        copy.wait()


def call(kernel, outs, args, places, scratch):
    args = [
        pltpu.with_memory_space_constraint(a, p) if p is HBM else a for a, p in zip(args, places)
    ]
    return pl.pallas_call(
        kernel,
        out_shape=[jax.ShapeDtypeStruct(o[0], (o + (jnp.float32,))[2]) for o in outs],
        in_specs=[pl.BlockSpec(memory_space=p) for p in places],
        out_specs=[pl.BlockSpec(memory_space=p) for p in (o[1] for o in outs)],
        scratch_shapes=[VMEM(s, jnp.float32) if isinstance(s, tuple) else s for s in scratch],
        compiler_params=pltpu.CompilerParams(vmem_limit_bytes=VMEM_LIMIT),
    )(*args)


def shards(
    rhs, diag_block, diag_inverse, lower_coef, upper_coef, side_coef, lower_cols, upper_cols, counts
):
    blocks, nvars, nrhs, cells = rhs.shape
    n = lax.axis_size("chain")
    inv = jnp.transpose(diag_inverse, (1, 2, 0, 3))
    low, upp, side = (
        jnp.transpose(a, (0, 2, 3, 1, 4)).reshape(-1, cells)
        for a in (lower_coef, upper_coef, side_coef)
    )
    lcols, ucols, used = lower_cols.T, upper_cols.T, counts.T
    m = lax.axis_size("sub")
    rows = blocks + REACH + 1
    half = n // 2
    parts = -(-len(column_order(nrhs)) // half)
    back = -(-32 // half)
    packed = min(8, half)
    extra = 8 // packed
    wide = 2 * (extra + WIDE // packed)
    sides = [list(range(half)), list(range(half, n))]
    tile = (nrhs, cells)

    mats = (VARS, VARS, SLOTS, blocks + PAD, cells)
    padded = (low.shape[0] + PAD, cells)

    count = half if half <= DIRECT else 1

    def pieces(pages):
        return [((pages,) + tile, VMEM)] * count if count > 1 else [((half, pages) + tile, VMEM)]

    def whole(pages):
        return [(half, pages) + tile] if count > 1 else []

    *maps, source, mlow, mupp, lcols, ucols, used = call(
        functools.partial(parted, functools.partial(local_kernel, half), 7, count, half),
        pieces(parts)
        + [(rhs.shape, VMEM), (mats, VMEM), (mats, VMEM)]
        + [(lcols.shape, VMEM, jnp.int32)] * 3,
        (rhs, inv, low, upp, lcols, ucols, used),
        (HBM,) * 7,
        [rhs.shape, (VARS, VARS, blocks + PAD, cells), low.shape, upp.shape]
        + [pltpu.SMEM(lcols.shape, jnp.int32)] * 3
        + [(rows, VARS, nrhs + WIDE, cells), (rows, VARS, nrhs + 2 * WIDE, cells)]
        + [(WIDE * SPACE, cells), pltpu.SemaphoreType.DMA((10,))]
        + whole(parts),
    )
    maps = exchange(maps, half, sides)
    cols, ends, offer = call(
        functools.partial(joined, first_solve_kernel, count, half),
        [
            ((half * COLUMNS * 8, cells), VMEM),
            ((half, 4 * extra) + tile, VMEM),
            ((wide,) + tile, VMEM),
        ],
        tuple(maps),
        (VMEM,) * count,
        [(half, wide) + tile, (wide // 2 * WIDE + PAD, cells)] + whole(parts),
    )
    got = lax.ppermute(
        offer, "chain", [p for i in range(half) for p in ((i, i + half), (i + half, i))]
    )
    states = call(
        functools.partial(parted, second_solve_kernel, 4, count, half),
        pieces(back),
        (cols, ends, offer, got),
        (VMEM,) * 4,
        [(half, 2 * extra) + tile, (extra * WIDE + PAD, cells), (half, 4 * extra) + tile]
        + whole(back),
    )
    states = exchange(states, half, sides)
    z, w, tail, edge, low, side = call(
        functools.partial(joined, functools.partial(sweep_kernel, half), count, half),
        [
            (rhs.shape, VMEM),
            ((blocks + 1, VARS) + tile, VMEM),
            ((REACH, VARS) + tile, VMEM),
            ((VARS,) + tile, VMEM),
            (padded, VMEM),
            (padded, VMEM),
        ],
        (*states, source, mlow, mupp, lcols, ucols, used, low, side),
        (VMEM,) * (3 + count) + (SMEM,) * 3 + (HBM,) * 2,
        [rhs.shape, (32 * 8, cells), pltpu.SemaphoreType.DMA((2,))] + whole(back),
    )
    tail = lax.ppermute(tail, "chain", [(i, (i + 1) % n) for i in range(n)])
    swap_a, swap_b = (
        lax.ppermute(edge, "sub", [p for i, j in pairs for p in ((i, j), (j, i))])
        for pairs in (
            [(i, i + 1) for i in range(0, m - 1, 2)],
            [(i, i + 1) for i in range(1, m - 1, 2)] + [(0, m - 1)] * (m % 2 == 0),
        )
    )
    inner, coef, correction = call(
        inner_kernel,
        [
            (rhs.shape, VMEM),
            ((-(-VARS * VARS * SLOTS // 8),) + (8, cells), VMEM),
            (rhs.shape, HBM),
        ],
        (z, w, low, side, lcols, used),
        (VMEM,) * 4 + (SMEM,) * 2,
        [(2 * REACH + 1, VARS) + tile, pltpu.SemaphoreType.DMA],
    )
    resid, squares = call(
        outer_kernel,
        [(rhs.shape, VMEM), ((n * m, 1, cells), VMEM)],
        (inner, coef, low, tail, swap_a, swap_b, lcols, used),
        (VMEM,) * 6 + (SMEM,) * 2,
        [(REACH + 1, VARS) + tile],
    )
    squares = lax.all_to_all(squares, ("chain", "sub"), 0, 0, tiled=True)
    entries = blocks * VARS * cells * n * m
    (residual_unit,) = call(
        functools.partial(scale_kernel, entries),
        [(rhs.shape, HBM)],
        (resid, squares),
        (VMEM, VMEM),
        [rhs.shape, pltpu.SemaphoreType.DMA((4 if blocks % 4 == 0 else 1,))],
    )
    return (correction, residual_unit)


def solution(mesh):
    in_specs = (
        P("chain", None, None, "sub"),
        P("chain", None, None, "sub"),
        P("chain", None, None, "sub"),
        P("chain", None, None, None, "sub"),
        P("chain", None, None, None, "sub"),
        P("chain", None, None, None, "sub"),
        P("chain", None),
        P("chain", None),
        P("chain", None),
    )
    out_specs = (P("chain", None, None, "sub"), P("chain", None, None, "sub"))
    return jax.shard_map(shards, mesh=mesh, in_specs=in_specs, out_specs=out_specs, check_vma=False)
```

profile of v0, /device:TPU:0, one launch (start us, length us, event | category | flops | bytes accessed | tf_op | source)
XLA Modules:
  0.0 52.5 jit_solution(2629941816360890417)
XLA Ops:
  0.6 6.0 %shard_map.95 = (f32[30,8,128]{2,1,0:T(8,128)S(1)}, f32[30,8,128]{2,1,0:T(8,128)S(1)}, f32[30,8,128]{2,1,0:T(8,128)S(1)}, f32[30,8,128]{2,1,0:T(8,128)S(1)}, f32...) custom-call(f32[24,5,8,128]{3,2,1,0:T(8,128)} %refs_0_.1, ...), custom_call_target="tpu_custom_call" | custom-call | tf_op jit(solution)/shard_map/pallas_call | solution.py:739
  6.6 3.0 %collective-permute-start = (f32[30,8,128]{2,1,0:T(8,128)S(1)}, f32[30,8,128]{2,1,0:T(8,128)S(1)}, u32[]{:S(2)}, u32[]{:S(2)}) collective-permute-start(f32[30,8,128]{2,1,0:T(8,128)S(1)} %get-tuple-element.31), channel_id=1, source_target_pairs={{0,4},{4,0},{8,12},{12,8},{16,20},{20,16},{24,28},{28,24},{1,5},{5... | collective-permute-start | bytes 368648 | tf_op jit(solution)/shard_map/ppermute | solution.py:197
  9.7 1.6 %collective-permute-start.1 = (f32[30,8,128]{2,1,0:T(8,128)S(1)}, f32[30,8,128]{2,1,0:T(8,128)S(1)}, u32[]{:S(2)}, u32[]{:S(2)}) collective-permute-start(f32[30,8,128]{2,1,0:T(8,128)S(1)} %get-tuple-element.32), channel_id=1, source_target_pairs={{0,8},{4,12},{8,0},{12,4},{16,24},{20,28},{24,16},{28,20},{1,9},{5... | collective-permute-start | bytes 368648 | tf_op jit(solution)/shard_map/ppermute | solution.py:197
  11.2 1.8 %collective-permute-done.refs_1_ = f32[30,8,128]{2,1,0:T(8,128)S(1)} collective-permute-done((f32[30,8,128]{2,1,0:T(8,128)S(1)}, f32[30,8,128]{2,1,0:T(8,128)S(1)}, u32[]{:S(2)}, u32[]{:S(2)}) %collective-permute-start) | collective-permute-done | bytes 122912 | tf_op jit(solution)/shard_map/ppermute | solution.py:197
  13.0 2.8 %collective-permute-done.1.refs_2_ = f32[30,8,128]{2,1,0:T(8,128)S(1)} collective-permute-done((f32[30,8,128]{2,1,0:T(8,128)S(1)}, f32[30,8,128]{2,1,0:T(8,128)S(1)}, u32[]{:S(2)}, u32[]{:S(2)}) %collective-permute-start.1) | collective-permute-done | bytes 122912 | tf_op jit(solution)/shard_map/ppermute | solution.py:197
  15.8 1.2 %collective-permute-done.2.refs_3_ = f32[30,8,128]{2,1,0:T(8,128)S(1)} collective-permute-done((f32[30,8,128]{2,1,0:T(8,128)S(1)}, f32[30,8,128]{2,1,0:T(8,128)S(1)}, u32[]{:S(2)}, u32[]{:S(2)}) %collective-permute-start.2) | collective-permute-done | bytes 122912 | tf_op jit(solution)/shard_map/ppermute | solution.py:197
  17.0 1.3 %shard_map.96 = (f32[2816,128]{1,0:T(8,128)S(1)}, f32[4,8,8,128]{3,2,1,0:T(8,128)S(1)}, f32[12,8,128]{2,1,0:T(8,128)S(1)}) custom-call(f32[30,8,128]{2,1,0:T(8,128)S(1)} %get-tuple-element.30.refs_0_, f32[30,8,128]{2,1,0:T(8,128)S(1)} %collective-permute-done.refs_1_, f32[30,8,128]{2,1,0:T(8,128)S(1)} %collective-permute-done.1.refs_2_, ...), custom_call_target="tpu_custom_call" | custom-call | tf_op jit(solution)/shard_map/pallas_call | solution.py:739
  18.3 2.8 %collective-permute-start.3 = (f32[12,8,128]{2,1,0:T(8,128)S(1)}, f32[12,8,128]{2,1,0:T(8,128)S(1)}, u32[]{:S(2)}, u32[]{:S(2)}) collective-permute-start(f32[12,8,128]{2,1,0:T(8,128)S(1)} %get-tuple-element.36.refs_2_), channel_id=1, source_target_pairs={{0,16},{16,0},{4,20},{20,4},{8,24},{24,8},{12,28},{28,12},{1,17},{... | collective-permute-start | bytes 147464 | tf_op jit(solution)/shard_map/ppermute | solution.py:807
  21.1 2.3 %collective-permute-done.3.refs_3_ = f32[12,8,128]{2,1,0:T(8,128)S(1)} collective-permute-done((f32[12,8,128]{2,1,0:T(8,128)S(1)}, f32[12,8,128]{2,1,0:T(8,128)S(1)}, u32[]{:S(2)}, u32[]{:S(2)}) %collective-permute-start.3) | collective-permute-done | bytes 49184 | tf_op jit(solution)/shard_map/ppermute | solution.py:807
  23.4 0.3 shard_map.97
  23.7 1.6 %collective-permute-start.4 = (f32[8,8,128]{2,1,0:T(8,128)S(1)}, f32[8,8,128]{2,1,0:T(8,128)S(1)}, u32[]{:S(2)}, u32[]{:S(2)}) collective-permute-start(f32[8,8,128]{2,1,0:T(8,128)S(1)} %get-tuple-element.38), channel_id=1, source_target_pairs={{0,4},{4,0},{8,12},{12,8},{16,20},{20,16},{24,28},{28,24},{1,5},{5... | collective-permute-start | bytes 98312 | tf_op jit(solution)/shard_map/ppermute | solution.py:197
  25.3 1.6 %collective-permute-start.5 = (f32[8,8,128]{2,1,0:T(8,128)S(1)}, f32[8,8,128]{2,1,0:T(8,128)S(1)}, u32[]{:S(2)}, u32[]{:S(2)}) collective-permute-start(f32[8,8,128]{2,1,0:T(8,128)S(1)} %get-tuple-element.39), channel_id=1, source_target_pairs={{0,8},{4,12},{8,0},{12,4},{16,24},{20,28},{24,16},{28,20},{1,9},{5... | collective-permute-start | bytes 98312 | tf_op jit(solution)/shard_map/ppermute | solution.py:197
  26.8 0.4 collective-permute-start.6
  27.2 0.4 collective-permute-done.4.refs_1_
  27.7 1.5 %collective-permute-done.5.refs_2_ = f32[8,8,128]{2,1,0:T(8,128)S(1)} collective-permute-done((f32[8,8,128]{2,1,0:T(8,128)S(1)}, f32[8,8,128]{2,1,0:T(8,128)S(1)}, u32[]{:S(2)}, u32[]{:S(2)}) %collective-permute-start.5) | collective-permute-done | bytes 32800 | tf_op jit(solution)/shard_map/ppermute | solution.py:197
  29.2 2.5 %collective-permute-done.6.refs_3_ = f32[8,8,128]{2,1,0:T(8,128)S(1)} collective-permute-done((f32[8,8,128]{2,1,0:T(8,128)S(1)}, f32[8,8,128]{2,1,0:T(8,128)S(1)}, u32[]{:S(2)}, u32[]{:S(2)}) %collective-permute-start.6) | collective-permute-done | bytes 32800 | tf_op jit(solution)/shard_map/ppermute | solution.py:197
  31.6 2.3 %shard_map.98 = (f32[24,5,8,128]{3,2,1,0:T(8,128)S(1)}, f32[25,5,8,128]{3,2,1,0:T(8,128)S(1)}, f32[3,5,8,128]{3,2,1,0:T(8,128)S(1)}, f32[5,8,128]{2,1,0:T(8,128)...) custom-call(f32[8,8,128]{2,1,0:T(8,128)S(1)} %get-tuple-element.37.refs_0_, ...), custom_call_target="tpu_custom_call" | custom-call | tf_op jit(solution)/shard_map/pallas_call | solution.py:739
  33.9 0.6 %collective-permute-start.7 = (f32[3,5,8,128]{3,2,1,0:T(8,128)S(1)}, f32[3,5,8,128]{3,2,1,0:T(8,128)S(1)}, u32[]{:S(2)}, u32[]{:S(2)}) collective-permute-start(f32[3,5,8,128]{3,2,1,0:T(8,128)S(1)} %get-tuple-element.54), channel_id=1, source_target_pairs={{0,4},{4,8},{8,12},{12,16},{16,20},{20,24},{24,28},{28,0},{1,5},{5... | collective-permute-start | bytes 184328 | tf_op jit(solution)/shard_map/ppermute | solution.py:833
  34.5 1.6 %collective-permute-start.8 = (f32[5,8,128]{2,1,0:T(8,128)S(1)}, f32[5,8,128]{2,1,0:T(8,128)S(1)}, u32[]{:S(2)}, u32[]{:S(2)}) collective-permute-start(f32[5,8,128]{2,1,0:T(8,128)S(1)} %get-tuple-element.55), channel_id=1, source_target_pairs={{0,1},{1,0},{2,3},{3,2},{4,5},{5,4},{6,7},{7,6},{8,9},{9,8},{10,11... | collective-permute-start | bytes 61448 | tf_op jit(solution)/shard_map/ppermute | solution.py:835
  36.1 1.5 %shard_map.99 = (f32[24,5,8,128]{3,2,1,0:T(8,128)S(1)}, f32[7,8,128]{2,1,0:T(8,128)S(1)}, f32[24,5,8,128]{3,2,1,0:T(8,128)}) custom-call(f32[24,5,8,128]{3,2,1,0:T(8,128)S(1)} %get-tuple-element.47.z, f32[25,5,8,128]{3,2,1,0:T(8,128)S(1)} %get-tuple-element.48.w, f32[1208,128]{1,0:T(8,128)S(1)} %get-tuple-element.49.low, ...), custom_call_target="tpu_custom_call" | custom-call | tf_op jit(solution)/shard_map/pallas_call | solution.py:739
  37.9 3.0 %collective-permute-done.7.tail = f32[3,5,8,128]{3,2,1,0:T(8,128)S(1)} collective-permute-done((f32[3,5,8,128]{3,2,1,0:T(8,128)S(1)}, f32[3,5,8,128]{3,2,1,0:T(8,128)S(1)}, u32[]{:S(2)}, u32[]{:S(2)}) %collective-permute-start.7) | collective-permute-done | bytes 61472 | tf_op jit(solution)/shard_map/ppermute | solution.py:833
  40.9 1.1 %shard_map.100 = (f32[24,5,8,128]{3,2,1,0:T(8,128)S(1)}, f32[32,1,128]{2,1,0:T(1,128)S(1)}) custom-call(f32[24,5,8,128]{3,2,1,0:T(8,128)S(1)} %get-tuple-element.52.inner, f32[7,8,128]{2,1,0:T(8,128)S(1)} %get-tuple-element.53.coef, f32[1208,128]{1,0:T(8,128)S(1)} %get-tuple-element.49.low, f32[3,5,8,128]{3,2,1,0:T(8,128)S(1)} %collective-permute-done.7.tail, ...), custom_call_target="tpu_custom_call" | custom-call | tf_op jit(solution)/shard_map/pallas_call | solution.py:739
  42.1 9.5 %all_to_all.5.squares = f32[32,1,128]{2,1,0:T(1,128)S(1)} all-to-all(f32[32,1,128]{2,1,0:T(1,128)S(1)} %get-tuple-element.57), channel_id=1, replica_groups=mesh['chain'=8,'sub'=4] {'chain','sub'}, dimensions={0} | all-to-all | bytes 32768 | tf_op jit(solution)/shard_map/all_to_all | solution.py:859
  51.5 0.9 %shard_map.101 = f32[24,5,8,128]{3,2,1,0:T(8,128)} custom-call(f32[24,5,8,128]{3,2,1,0:T(8,128)S(1)} %get-tuple-element.56.resid, f32[32,1,128]{2,1,0:T(1,128)S(1)} %all_to_all.5.squares), custom_call_target="tpu_custom_call" | custom-call | tf_op jit(solution)/shard_map/pallas_call | solution.py:739
  (4 shorter events, 0.3 us)
Async XLA Ops:
  6.6 6.4 %collective-permute-start = (f32[30,8,128]{2,1,0:T(8,128)S(1)}, f32[30,8,128]{2,1,0:T(8,128)S(1)}, u32[]{:S(2)}, u32[]{:S(2)}) collective-permute-start(f32[30,8,128]{2,1,0:T(8,128)S(1)} %get-tuple-element.31), channel_id=1, source_target_pairs={{0,4},{4,0},{8,12},{12,8},{16,20},{20,16},{24,28},{28,24},{1,5},{5... | collective-permute-start | bytes 368648 | tf_op jit(solution)/shard_map/ppermute | solution.py:197
  9.7 6.1 %collective-permute-start.1 = (f32[30,8,128]{2,1,0:T(8,128)S(1)}, f32[30,8,128]{2,1,0:T(8,128)S(1)}, u32[]{:S(2)}, u32[]{:S(2)}) collective-permute-start(f32[30,8,128]{2,1,0:T(8,128)S(1)} %get-tuple-element.32), channel_id=1, source_target_pairs={{0,8},{4,12},{8,0},{12,4},{16,24},{20,28},{24,16},{28,20},{1,9},{5... | collective-permute-start | bytes 368648 | tf_op jit(solution)/shard_map/ppermute | solution.py:197
  11.2 5.8 %collective-permute-start.2 = (f32[30,8,128]{2,1,0:T(8,128)S(1)}, f32[30,8,128]{2,1,0:T(8,128)S(1)}, u32[]{:S(2)}, u32[]{:S(2)}) collective-permute-start(f32[30,8,128]{2,1,0:T(8,128)S(1)} %get-tuple-element.33), channel_id=1, source_target_pairs={{0,12},{4,8},{8,4},{12,0},{16,28},{20,24},{24,20},{28,16},{1,13},{... | collective-permute-start | bytes 368648 | tf_op jit(solution)/shard_map/ppermute | solution.py:197
  18.3 5.1 %collective-permute-start.3 = (f32[12,8,128]{2,1,0:T(8,128)S(1)}, f32[12,8,128]{2,1,0:T(8,128)S(1)}, u32[]{:S(2)}, u32[]{:S(2)}) collective-permute-start(f32[12,8,128]{2,1,0:T(8,128)S(1)} %get-tuple-element.36.refs_2_), channel_id=1, source_target_pairs={{0,16},{16,0},{4,20},{20,4},{8,24},{24,8},{12,28},{28,12},{1,17},{... | collective-permute-start | bytes 147464 | tf_op jit(solution)/shard_map/ppermute | solution.py:807
  23.7 4.0 %collective-permute-start.4 = (f32[8,8,128]{2,1,0:T(8,128)S(1)}, f32[8,8,128]{2,1,0:T(8,128)S(1)}, u32[]{:S(2)}, u32[]{:S(2)}) collective-permute-start(f32[8,8,128]{2,1,0:T(8,128)S(1)} %get-tuple-element.38), channel_id=1, source_target_pairs={{0,4},{4,0},{8,12},{12,8},{16,20},{20,16},{24,28},{28,24},{1,5},{5... | collective-permute-start | bytes 98312 | tf_op jit(solution)/shard_map/ppermute | solution.py:197
  25.3 3.9 %collective-permute-start.5 = (f32[8,8,128]{2,1,0:T(8,128)S(1)}, f32[8,8,128]{2,1,0:T(8,128)S(1)}, u32[]{:S(2)}, u32[]{:S(2)}) collective-permute-start(f32[8,8,128]{2,1,0:T(8,128)S(1)} %get-tuple-element.39), channel_id=1, source_target_pairs={{0,8},{4,12},{8,0},{12,4},{16,24},{20,28},{24,16},{28,20},{1,9},{5... | collective-permute-start | bytes 98312 | tf_op jit(solution)/shard_map/ppermute | solution.py:197
  26.8 4.8 %collective-permute-start.6 = (f32[8,8,128]{2,1,0:T(8,128)S(1)}, f32[8,8,128]{2,1,0:T(8,128)S(1)}, u32[]{:S(2)}, u32[]{:S(2)}) collective-permute-start(f32[8,8,128]{2,1,0:T(8,128)S(1)} %get-tuple-element.40), channel_id=1, source_target_pairs={{0,12},{4,8},{8,4},{12,0},{16,28},{20,24},{24,20},{28,16},{1,13},{... | collective-permute-start | bytes 98312 | tf_op jit(solution)/shard_map/ppermute | solution.py:197
  33.9 7.0 %collective-permute-start.7 = (f32[3,5,8,128]{3,2,1,0:T(8,128)S(1)}, f32[3,5,8,128]{3,2,1,0:T(8,128)S(1)}, u32[]{:S(2)}, u32[]{:S(2)}) collective-permute-start(f32[3,5,8,128]{3,2,1,0:T(8,128)S(1)} %get-tuple-element.54), channel_id=1, source_target_pairs={{0,4},{4,8},{8,12},{12,16},{16,20},{20,24},{24,28},{28,0},{1,5},{5... | collective-permute-start | bytes 184328 | tf_op jit(solution)/shard_map/ppermute | solution.py:833
  34.5 3.4 %collective-permute-start.9 = (f32[5,8,128]{2,1,0:T(8,128)S(1)}, f32[5,8,128]{2,1,0:T(8,128)S(1)}, u32[]{:S(2)}, u32[]{:S(2)}) collective-permute-start(f32[5,8,128]{2,1,0:T(8,128)S(1)} %get-tuple-element.55), channel_id=1, source_target_pairs={{1,2},{2,1},{0,3},{3,0},{5,6},{6,5},{4,7},{7,4},{9,10},{10,9},{8,1... | collective-permute-start | bytes 61448 | tf_op jit(solution)/shard_map/ppermute | solution.py:835
  34.5 3.4 %collective-permute-start.8 = (f32[5,8,128]{2,1,0:T(8,128)S(1)}, f32[5,8,128]{2,1,0:T(8,128)S(1)}, u32[]{:S(2)}, u32[]{:S(2)}) collective-permute-start(f32[5,8,128]{2,1,0:T(8,128)S(1)} %get-tuple-element.55), channel_id=1, source_target_pairs={{0,1},{1,0},{2,3},{3,2},{4,5},{5,4},{6,7},{7,6},{8,9},{9,8},{10,11... | collective-permute-start | bytes 61448 | tf_op jit(solution)/shard_map/ppermute | solution.py:835
where the time goes:
time: 52.6 us; the launch traced here: 52.5 us
  waiting for transfers between devices  15.8 us (30%)
  Pallas kernels  13.5 us (26%)
  starting transfers between devices  13.1 us (25%)
  blocking collectives  9.46 us (18%)
  between operations  0.69 us (1%)
    pallas_call x7, Pallas kernels, call(): pl.pallas_call(kernel, out_shape=[jax.ShapeDtypeStruct(o[0], (o + (jnp.fl...  13.5 us
    ppermute x6, waiting for transfers between devices, exchange(): lax.ppermute(parts[x], 'chain', [(i, i ^ x) for i in range(count)])  10.2 us
    all_to_all x1, blocking collectives, shards(): squares = lax.all_to_all(squares, ('chain', 'sub'), 0, 0, tiled=True)  9.46 us
    ppermute x6, starting transfers between devices, exchange(): lax.ppermute(parts[x], 'chain', [(i, i ^ x) for i in range(count)])  8.16 us
    ppermute x1, waiting for transfers between devices, shards(): tail = lax.ppermute(tail, 'chain', [(i, (i + 1) % n) for i in range(n)])  3.02 us
    ppermute x1, starting transfers between devices, shards(): lax.ppermute(offer, 'chain', [p for i in range(half) for p in ((i, i + ha...  2.76 us
    ppermute x1, waiting for transfers between devices, shards(): lax.ppermute(offer, 'chain', [p for i in range(half) for p in ((i, i + ha...  2.29 us
    ppermute x2, starting transfers between devices, shards(): lax.ppermute(edge, 'sub', [p for i, j in pairs for p in ((i, j), (j, i))])  1.61 us
  transfers between devices with their start and end apart: 10, of which 9 were waited for; matrix products, arithmetic and copies ran while one was open for 0% of the time, Pallas kernels for 3%

commit v1 on v0

--- a/solution.py
+++ b/solution.py
@@ -159,16 +159,20 @@
     return lax.axis_index("chain") % n
 
 
+def distances(count):
+    return [0, count - 1] + list(range(1, count - 1))
+
+
 def gather_parts(parts, buf):
     here = position(buf.shape[0])
-    for x, part in enumerate(parts):
+    for x, part in zip(distances(len(parts)), parts):
         for page in range(part.shape[0]):
             buf[here ^ x, page] = part[page]
 
 
 def scatter_parts(buf, parts):
     here = position(buf.shape[0])
-    for x, part in enumerate(parts):
+    for x, part in zip(distances(len(parts)), parts):
         for page in range(part.shape[0]):
             part[page] = buf[here ^ x, page]
 
@@ -192,10 +196,10 @@
     if len(parts) == 1:
         return [lax.all_to_all(parts[0], "chain", 0, 0, tiled=True, axis_index_groups=groups)]
     count = lax.axis_size("chain")
-    parts = list(parts)
-    for x in [len(parts) - 1] + list(range(1, len(parts) - 1)):
-        parts[x] = lax.ppermute(parts[x], "chain", [(i, i ^ x) for i in range(count)])
-    return parts
+    return [
+        part if x == 0 else lax.ppermute(part, "chain", [(i, i ^ x) for i in range(count)])
+        for x, part in zip(distances(len(parts)), parts)
+    ]
 
 
 def local_kernel(

time: 52.6 us -> 51.5 us (0.979)
  waiting for transfers between devices: 15.8 us -> 14.4 us
    ppermute x6, waiting for transfers between devices: 10.2 us -> 8.47 us  [exchange(): lax.ppermute(part, 'chain', [(i, i ^ x) for i in range(count)])]
    ppermute x1, waiting for transfers between devices: 2.29 us -> 2.91 us  [shards(): lax.ppermute(offer, 'chain', [p for i in range(half) for p in ((i, i + ha...]
where the time goes in v1:
time: 51.5 us; the launch traced here: 51.3 us
  waiting for transfers between devices  14.4 us (28%)
  Pallas kernels  13.5 us (26%)
  starting transfers between devices  13.3 us (26%)
  blocking collectives  9.42 us (18%)
  between operations  0.69 us (1%)
    pallas_call x7, Pallas kernels, call(): pl.pallas_call(kernel, out_shape=[jax.ShapeDtypeStruct(o[0], (o + (jnp.fl...  13.5 us
    all_to_all x1, blocking collectives, shards(): squares = lax.all_to_all(squares, ('chain', 'sub'), 0, 0, tiled=True)  9.42 us
    ppermute x6, waiting for transfers between devices, exchange(): lax.ppermute(part, 'chain', [(i, i ^ x) for i in range(count)])  8.47 us
    ppermute x6, starting transfers between devices, exchange(): lax.ppermute(part, 'chain', [(i, i ^ x) for i in range(count)])  8.24 us
    ppermute x1, waiting for transfers between devices, shards(): lax.ppermute(offer, 'chain', [p for i in range(half) for p in ((i, i + ha...  2.91 us
    ppermute x1, waiting for transfers between devices, shards(): tail = lax.ppermute(tail, 'chain', [(i, (i + 1) % n) for i in range(n)])  2.86 us
    ppermute x1, starting transfers between devices, shards(): lax.ppermute(offer, 'chain', [p for i in range(half) for p in ((i, i + ha...  2.66 us
    ppermute x2, starting transfers between devices, shards(): lax.ppermute(edge, 'sub', [p for i, j in pairs for p in ((i, j), (j, i))])  1.64 us
  transfers between devices with their start and end apart: 10, of which 9 were waited for; matrix products, arithmetic and copies ran while one was open for 0% of the time, Pallas kernels for 3%

profile of v1, /device:TPU:0, one launch (start us, length us, event | category | flops | bytes accessed | tf_op | source)
XLA Modules:
  0.0 51.3 jit_solution(7995874223451116444)
XLA Ops:
  0.6 6.0 %shard_map.95 = (f32[30,8,128]{2,1,0:T(8,128)S(1)}, f32[30,8,128]{2,1,0:T(8,128)S(1)}, f32[30,8,128]{2,1,0:T(8,128)S(1)}, f32[30,8,128]{2,1,0:T(8,128)S(1)}, f32...) custom-call(f32[24,5,8,128]{3,2,1,0:T(8,128)} %refs_0_.1, ...), custom_call_target="tpu_custom_call" | custom-call | tf_op jit(solution)/shard_map/pallas_call | solution.py:743
  6.6 4.0 %collective-permute-start = (f32[30,8,128]{2,1,0:T(8,128)S(1)}, f32[30,8,128]{2,1,0:T(8,128)S(1)}, u32[]{:S(2)}, u32[]{:S(2)}) collective-permute-start(f32[30,8,128]{2,1,0:T(8,128)S(1)} %get-tuple-element.31), channel_id=1, source_target_pairs={{0,12},{4,8},{8,4},{12,0},{16,28},{20,24},{24,20},{28,16},{1,13},{... | collective-permute-start | bytes 368648 | tf_op jit(solution)/shard_map/ppermute | solution.py:200
  10.7 0.5 collective-permute-start.1
  11.3 3.1 %collective-permute-done.refs_1_ = f32[30,8,128]{2,1,0:T(8,128)S(1)} collective-permute-done((f32[30,8,128]{2,1,0:T(8,128)S(1)}, f32[30,8,128]{2,1,0:T(8,128)S(1)}, u32[]{:S(2)}, u32[]{:S(2)}) %collective-permute-start) | collective-permute-done | bytes 122912 | tf_op jit(solution)/shard_map/ppermute | solution.py:200
  14.4 2.2 %collective-permute-done.1.refs_2_ = f32[30,8,128]{2,1,0:T(8,128)S(1)} collective-permute-done((f32[30,8,128]{2,1,0:T(8,128)S(1)}, f32[30,8,128]{2,1,0:T(8,128)S(1)}, u32[]{:S(2)}, u32[]{:S(2)}) %collective-permute-start.1) | collective-permute-done | bytes 122912 | tf_op jit(solution)/shard_map/ppermute | solution.py:200
  16.8 1.3 %shard_map.96 = (f32[2816,128]{1,0:T(8,128)S(1)}, f32[4,8,8,128]{3,2,1,0:T(8,128)S(1)}, f32[12,8,128]{2,1,0:T(8,128)S(1)}) custom-call(f32[30,8,128]{2,1,0:T(8,128)S(1)} %get-tuple-element.30.refs_0_, f32[30,8,128]{2,1,0:T(8,128)S(1)} %collective-permute-done.refs_1_, f32[30,8,128]{2,1,0:T(8,128)S(1)} %collective-permute-done.1.refs_2_, ...), custom_call_target="tpu_custom_call" | custom-call | tf_op jit(solution)/shard_map/pallas_call | solution.py:743
  18.1 2.7 %collective-permute-start.3 = (f32[12,8,128]{2,1,0:T(8,128)S(1)}, f32[12,8,128]{2,1,0:T(8,128)S(1)}, u32[]{:S(2)}, u32[]{:S(2)}) collective-permute-start(f32[12,8,128]{2,1,0:T(8,128)S(1)} %get-tuple-element.36.refs_2_), channel_id=1, source_target_pairs={{0,16},{16,0},{4,20},{20,4},{8,24},{24,8},{12,28},{28,12},{1,17},{... | collective-permute-start | bytes 147464 | tf_op jit(solution)/shard_map/ppermute | solution.py:811
  20.8 2.9 %collective-permute-done.3.refs_3_ = f32[12,8,128]{2,1,0:T(8,128)S(1)} collective-permute-done((f32[12,8,128]{2,1,0:T(8,128)S(1)}, f32[12,8,128]{2,1,0:T(8,128)S(1)}, u32[]{:S(2)}, u32[]{:S(2)}) %collective-permute-start.3) | collective-permute-done | bytes 49184 | tf_op jit(solution)/shard_map/ppermute | solution.py:811
  23.7 0.3 shard_map.97
  24.0 1.3 %collective-permute-start.4 = (f32[8,8,128]{2,1,0:T(8,128)S(1)}, f32[8,8,128]{2,1,0:T(8,128)S(1)}, u32[]{:S(2)}, u32[]{:S(2)}) collective-permute-start(f32[8,8,128]{2,1,0:T(8,128)S(1)} %get-tuple-element.38), channel_id=1, source_target_pairs={{0,12},{4,8},{8,4},{12,0},{16,28},{20,24},{24,20},{28,16},{1,13},{... | collective-permute-start | bytes 98312 | tf_op jit(solution)/shard_map/ppermute | solution.py:200
  25.3 1.3 %collective-permute-start.5 = (f32[8,8,128]{2,1,0:T(8,128)S(1)}, f32[8,8,128]{2,1,0:T(8,128)S(1)}, u32[]{:S(2)}, u32[]{:S(2)}) collective-permute-start(f32[8,8,128]{2,1,0:T(8,128)S(1)} %get-tuple-element.39), channel_id=1, source_target_pairs={{0,4},{4,0},{8,12},{12,8},{16,20},{20,16},{24,28},{28,24},{1,5},{5... | collective-permute-start | bytes 98312 | tf_op jit(solution)/shard_map/ppermute | solution.py:200
  26.6 0.9 %collective-permute-start.6 = (f32[8,8,128]{2,1,0:T(8,128)S(1)}, f32[8,8,128]{2,1,0:T(8,128)S(1)}, u32[]{:S(2)}, u32[]{:S(2)}) collective-permute-start(f32[8,8,128]{2,1,0:T(8,128)S(1)} %get-tuple-element.40), channel_id=1, source_target_pairs={{0,8},{4,12},{8,0},{12,4},{16,24},{20,28},{24,16},{28,20},{1,9},{5... | collective-permute-start | bytes 98312 | tf_op jit(solution)/shard_map/ppermute | solution.py:200
  27.5 1.3 %collective-permute-done.4.refs_1_ = f32[8,8,128]{2,1,0:T(8,128)S(1)} collective-permute-done((f32[8,8,128]{2,1,0:T(8,128)S(1)}, f32[8,8,128]{2,1,0:T(8,128)S(1)}, u32[]{:S(2)}, u32[]{:S(2)}) %collective-permute-start.4) | collective-permute-done | bytes 32800 | tf_op jit(solution)/shard_map/ppermute | solution.py:200
  28.9 0.4 collective-permute-done.5.refs_2_
  29.2 1.3 %collective-permute-done.6.refs_3_ = f32[8,8,128]{2,1,0:T(8,128)S(1)} collective-permute-done((f32[8,8,128]{2,1,0:T(8,128)S(1)}, f32[8,8,128]{2,1,0:T(8,128)S(1)}, u32[]{:S(2)}, u32[]{:S(2)}) %collective-permute-start.6) | collective-permute-done | bytes 32800 | tf_op jit(solution)/shard_map/ppermute | solution.py:200
  30.5 2.3 %shard_map.98 = (f32[24,5,8,128]{3,2,1,0:T(8,128)S(1)}, f32[25,5,8,128]{3,2,1,0:T(8,128)S(1)}, f32[3,5,8,128]{3,2,1,0:T(8,128)S(1)}, f32[5,8,128]{2,1,0:T(8,128)...) custom-call(f32[8,8,128]{2,1,0:T(8,128)S(1)} %get-tuple-element.37.refs_0_, ...), custom_call_target="tpu_custom_call" | custom-call | tf_op jit(solution)/shard_map/pallas_call | solution.py:743
  32.8 0.8 %collective-permute-start.7 = (f32[3,5,8,128]{3,2,1,0:T(8,128)S(1)}, f32[3,5,8,128]{3,2,1,0:T(8,128)S(1)}, u32[]{:S(2)}, u32[]{:S(2)}) collective-permute-start(f32[3,5,8,128]{3,2,1,0:T(8,128)S(1)} %get-tuple-element.54), channel_id=1, source_target_pairs={{0,4},{4,8},{8,12},{12,16},{16,20},{20,24},{24,28},{28,0},{1,5},{5... | collective-permute-start | bytes 184328 | tf_op jit(solution)/shard_map/ppermute | solution.py:837
  33.6 1.6 %collective-permute-start.8 = (f32[5,8,128]{2,1,0:T(8,128)S(1)}, f32[5,8,128]{2,1,0:T(8,128)S(1)}, u32[]{:S(2)}, u32[]{:S(2)}) collective-permute-start(f32[5,8,128]{2,1,0:T(8,128)S(1)} %get-tuple-element.55), channel_id=1, source_target_pairs={{0,1},{1,0},{2,3},{3,2},{4,5},{5,4},{6,7},{7,6},{8,9},{9,8},{10,11... | collective-permute-start | bytes 61448 | tf_op jit(solution)/shard_map/ppermute | solution.py:839
  35.2 1.5 %shard_map.99 = (f32[24,5,8,128]{3,2,1,0:T(8,128)S(1)}, f32[7,8,128]{2,1,0:T(8,128)S(1)}, f32[24,5,8,128]{3,2,1,0:T(8,128)}) custom-call(f32[24,5,8,128]{3,2,1,0:T(8,128)S(1)} %get-tuple-element.47.z, f32[25,5,8,128]{3,2,1,0:T(8,128)S(1)} %get-tuple-element.48.w, f32[1208,128]{1,0:T(8,128)S(1)} %get-tuple-element.49.low, ...), custom_call_target="tpu_custom_call" | custom-call | tf_op jit(solution)/shard_map/pallas_call | solution.py:743
  36.7 0.2 collective-permute-done.9.swap_b
  36.9 2.9 %collective-permute-done.7.tail = f32[3,5,8,128]{3,2,1,0:T(8,128)S(1)} collective-permute-done((f32[3,5,8,128]{3,2,1,0:T(8,128)S(1)}, f32[3,5,8,128]{3,2,1,0:T(8,128)S(1)}, u32[]{:S(2)}, u32[]{:S(2)}) %collective-permute-start.7) | collective-permute-done | bytes 61472 | tf_op jit(solution)/shard_map/ppermute | solution.py:837
  39.8 1.1 %shard_map.100 = (f32[24,5,8,128]{3,2,1,0:T(8,128)S(1)}, f32[32,1,128]{2,1,0:T(1,128)S(1)}) custom-call(f32[24,5,8,128]{3,2,1,0:T(8,128)S(1)} %get-tuple-element.52.inner, f32[7,8,128]{2,1,0:T(8,128)S(1)} %get-tuple-element.53.coef, f32[1208,128]{1,0:T(8,128)S(1)} %get-tuple-element.49.low, f32[3,5,8,128]{3,2,1,0:T(8,128)S(1)} %collective-permute-done.7.tail, ...), custom_call_target="tpu_custom_call" | custom-call | tf_op jit(solution)/shard_map/pallas_call | solution.py:743
  40.9 9.4 %all_to_all.5.squares = f32[32,1,128]{2,1,0:T(1,128)S(1)} all-to-all(f32[32,1,128]{2,1,0:T(1,128)S(1)} %get-tuple-element.57), channel_id=1, replica_groups=mesh['chain'=8,'sub'=4] {'chain','sub'}, dimensions={0} | all-to-all | bytes 32768 | tf_op jit(solution)/shard_map/all_to_all | solution.py:863
  50.4 0.9 %shard_map.101 = f32[24,5,8,128]{3,2,1,0:T(8,128)} custom-call(f32[24,5,8,128]{3,2,1,0:T(8,128)S(1)} %get-tuple-element.56.resid, f32[32,1,128]{2,1,0:T(1,128)S(1)} %all_to_all.5.squares), custom_call_target="tpu_custom_call" | custom-call | tf_op jit(solution)/shard_map/pallas_call | solution.py:743
  (4 shorter events, 0.3 us)
Async XLA Ops:
  6.6 7.8 %collective-permute-start = (f32[30,8,128]{2,1,0:T(8,128)S(1)}, f32[30,8,128]{2,1,0:T(8,128)S(1)}, u32[]{:S(2)}, u32[]{:S(2)}) collective-permute-start(f32[30,8,128]{2,1,0:T(8,128)S(1)} %get-tuple-element.31), channel_id=1, source_target_pairs={{0,12},{4,8},{8,4},{12,0},{16,28},{20,24},{24,20},{28,16},{1,13},{... | collective-permute-start | bytes 368648 | tf_op jit(solution)/shard_map/ppermute | solution.py:200
  10.7 6.0 %collective-permute-start.1 = (f32[30,8,128]{2,1,0:T(8,128)S(1)}, f32[30,8,128]{2,1,0:T(8,128)S(1)}, u32[]{:S(2)}, u32[]{:S(2)}) collective-permute-start(f32[30,8,128]{2,1,0:T(8,128)S(1)} %get-tuple-element.32), channel_id=1, source_target_pairs={{0,4},{4,0},{8,12},{12,8},{16,20},{20,16},{24,28},{28,24},{1,5},{5... | collective-permute-start | bytes 368648 | tf_op jit(solution)/shard_map/ppermute | solution.py:200
  11.2 5.6 %collective-permute-start.2 = (f32[30,8,128]{2,1,0:T(8,128)S(1)}, f32[30,8,128]{2,1,0:T(8,128)S(1)}, u32[]{:S(2)}, u32[]{:S(2)}) collective-permute-start(f32[30,8,128]{2,1,0:T(8,128)S(1)} %get-tuple-element.33), channel_id=1, source_target_pairs={{0,8},{4,12},{8,0},{12,4},{16,24},{20,28},{24,16},{28,20},{1,9},{5... | collective-permute-start | bytes 368648 | tf_op jit(solution)/shard_map/ppermute | solution.py:200
  18.1 5.6 %collective-permute-start.3 = (f32[12,8,128]{2,1,0:T(8,128)S(1)}, f32[12,8,128]{2,1,0:T(8,128)S(1)}, u32[]{:S(2)}, u32[]{:S(2)}) collective-permute-start(f32[12,8,128]{2,1,0:T(8,128)S(1)} %get-tuple-element.36.refs_2_), channel_id=1, source_target_pairs={{0,16},{16,0},{4,20},{20,4},{8,24},{24,8},{12,28},{28,12},{1,17},{... | collective-permute-start | bytes 147464 | tf_op jit(solution)/shard_map/ppermute | solution.py:811
  24.0 4.9 %collective-permute-start.4 = (f32[8,8,128]{2,1,0:T(8,128)S(1)}, f32[8,8,128]{2,1,0:T(8,128)S(1)}, u32[]{:S(2)}, u32[]{:S(2)}) collective-permute-start(f32[8,8,128]{2,1,0:T(8,128)S(1)} %get-tuple-element.38), channel_id=1, source_target_pairs={{0,12},{4,8},{8,4},{12,0},{16,28},{20,24},{24,20},{28,16},{1,13},{... | collective-permute-start | bytes 98312 | tf_op jit(solution)/shard_map/ppermute | solution.py:200
  25.3 3.9 %collective-permute-start.5 = (f32[8,8,128]{2,1,0:T(8,128)S(1)}, f32[8,8,128]{2,1,0:T(8,128)S(1)}, u32[]{:S(2)}, u32[]{:S(2)}) collective-permute-start(f32[8,8,128]{2,1,0:T(8,128)S(1)} %get-tuple-element.39), channel_id=1, source_target_pairs={{0,4},{4,0},{8,12},{12,8},{16,20},{20,16},{24,28},{28,24},{1,5},{5... | collective-permute-start | bytes 98312 | tf_op jit(solution)/shard_map/ppermute | solution.py:200
  26.6 3.9 %collective-permute-start.6 = (f32[8,8,128]{2,1,0:T(8,128)S(1)}, f32[8,8,128]{2,1,0:T(8,128)S(1)}, u32[]{:S(2)}, u32[]{:S(2)}) collective-permute-start(f32[8,8,128]{2,1,0:T(8,128)S(1)} %get-tuple-element.40), channel_id=1, source_target_pairs={{0,8},{4,12},{8,0},{12,4},{16,24},{20,28},{24,16},{28,20},{1,9},{5... | collective-permute-start | bytes 98312 | tf_op jit(solution)/shard_map/ppermute | solution.py:200
  32.8 7.0 %collective-permute-start.7 = (f32[3,5,8,128]{3,2,1,0:T(8,128)S(1)}, f32[3,5,8,128]{3,2,1,0:T(8,128)S(1)}, u32[]{:S(2)}, u32[]{:S(2)}) collective-permute-start(f32[3,5,8,128]{3,2,1,0:T(8,128)S(1)} %get-tuple-element.54), channel_id=1, source_target_pairs={{0,4},{4,8},{8,12},{12,16},{16,20},{20,24},{24,28},{28,0},{1,5},{5... | collective-permute-start | bytes 184328 | tf_op jit(solution)/shard_map/ppermute | solution.py:837
  33.6 3.4 %collective-permute-start.9 = (f32[5,8,128]{2,1,0:T(8,128)S(1)}, f32[5,8,128]{2,1,0:T(8,128)S(1)}, u32[]{:S(2)}, u32[]{:S(2)}) collective-permute-start(f32[5,8,128]{2,1,0:T(8,128)S(1)} %get-tuple-element.55), channel_id=1, source_target_pairs={{1,2},{2,1},{0,3},{3,0},{5,6},{6,5},{4,7},{7,4},{9,10},{10,9},{8,1... | collective-permute-start | bytes 61448 | tf_op jit(solution)/shard_map/ppermute | solution.py:839
  33.6 3.4 %collective-permute-start.8 = (f32[5,8,128]{2,1,0:T(8,128)S(1)}, f32[5,8,128]{2,1,0:T(8,128)S(1)}, u32[]{:S(2)}, u32[]{:S(2)}) collective-permute-start(f32[5,8,128]{2,1,0:T(8,128)S(1)} %get-tuple-element.55), channel_id=1, source_target_pairs={{0,1},{1,0},{2,3},{3,2},{4,5},{5,4},{6,7},{7,6},{8,9},{9,8},{10,11... | collective-permute-start | bytes 61448 | tf_op jit(solution)/shard_map/ppermute | solution.py:839

commit v2 on v1

--- a/solution.py
+++ b/solution.py
@@ -208,6 +208,7 @@
     inv_h,
     low_h,
     upp_h,
+    side_h,
     lcols_h,
     ucols_h,
     counts_h,
@@ -218,9 +219,10 @@
     lcols_v,
     ucols_v,
     counts_v,
+    low,
+    side,
     rhs,
     inv,
-    low,
     upp,
     lcols,
     ucols,
@@ -235,15 +237,16 @@
         for k, (src, dst) in enumerate(
             (
                 (inv_h, inv.at[:, :, pl.ds(0, rhs.shape[0]), :]),
-                (low_h, low),
+                (low_h, low.at[pl.ds(0, low_h.shape[0]), :]),
                 (lcols_h, lcols),
                 (counts_h, counts),
                 (ucols_h, ucols),
                 (rhs_h, rhs),
-                (upp_h, upp),
+                (upp_h, upp.at[pl.ds(0, upp_h.shape[0]), :]),
                 (lcols_h, lcols_v),
                 (ucols_h, ucols_v),
                 (counts_h, counts_v),
+                (side_h, side.at[pl.ds(0, side_h.shape[0]), :]),
             )
         )
     ]
@@ -285,7 +288,7 @@
         return carry
 
     steps(blocks, 6, first)
-    for copy in copies[6:]:
+    for copy in copies[6:-1]:
         copy.wait()
     products(inv, upp, mupp)
 
@@ -331,6 +334,7 @@
         items += [zero] * (n - len(items))
         for k, item in enumerate(block_transpose(items, width, cells)):
             out[k, page] = item
+    copies[-1].wait()
 
 
 def split(value, period, stop, width, cells):
@@ -508,38 +512,26 @@
     steps(n, 4, pack)
 
 
-def sweep_kernel(
-    n,
-    states,
-    source,
-    mlow,
-    mupp,
-    lcols,
-    ucols,
-    counts,
-    low_h,
-    side_h,
-    zout,
-    wout,
-    tail,
-    edge,
-    low,
-    side,
-    ybuf,
-    stage,
-    sems,
+def near_blocks(window, b, base, sign, cols, counts, side):
+    nears = []
+    for k in range(SLOTS):
+        off = sign * (cols[k, b] - base - b)
+        picks = []
+        for v in range(VARS):
+            value = window[(REACH - 1) * VARS + v]
+            for d in range(REACH - 1):
+                value = jnp.where(off == d + 1, window[d * VARS + v], value)
+            picks.append(value if k == 0 else jnp.where(k < counts[side, b], value, 0.0))
+        nears.append([[value] for value in picks])
+    return nears
+
+
+def forward_kernel(
+    n, states, source, mlow, mupp, lcols, ucols, counts, yout, start, tail, stage
 ):
-    total = low_h.shape[0]
-    copies = [
-        pltpu.make_async_copy(src, dst.at[pl.ds(0, total), :], sems.at[k])
-        for k, (src, dst) in enumerate(((low_h, low), (side_h, side)))
-    ]
-    for copy in copies:
-        copy.start()
     blocks, _, nrhs, cells = source.shape
     base = lax.axis_index("chain") * blocks
     width = cells // n
-    zero = jnp.zeros((nrhs, cells), jnp.float32)
     items = []
     for r in range(states.shape[1]):
         items += block_transpose([states[k, r] for k in range(n)], width, cells)
@@ -550,34 +542,37 @@
         rows = [stage[pl.ds(start + q // 8 * 64 + q % 8, 8, stride=8), :] for q in range(STATE)]
         return tuple(rows)
 
+    def first(b, window):
+        acc = couple(mlow, b, near_blocks(window, b, base, -1, lcols, counts, 0))
+        fresh = tuple(source[b, i] + acc[i][0] for i in range(VARS))
+        return Kept(fresh + window[: STATE - VARS], [(yout, (b, i), fresh[i]) for i in range(VARS)])
+
+    steps(blocks, 8, first, entering(0))
+
+    window = entering(128)
+    for q in range(STATE):
+        start[q] = window[q]
+    for m in reversed(range(REACH)):
+        c = blocks - REACH + m
+        acc = couple(mupp, c, near_blocks(window, c, base, 1, ucols, counts, 1))
+        fresh = tuple(yout[c, i] + acc[i][0] for i in range(VARS))
+        for i in range(VARS):
+            tail[m, i] = acc[i][0]
+        window = fresh + window[: STATE - VARS]
+
+
+def sweep_kernel(ybuf, start, mupp, ucols, counts, zout, wout, edge):
+    blocks, _, nrhs, cells = ybuf.shape
+    base = lax.axis_index("chain") * blocks
+    zero = jnp.zeros((nrhs, cells), jnp.float32)
     lane = lanes_of(cells)
     for v in range(VARS):
         wout[blocks, v] = zero
 
-    def near(window, b, sign, cols, side):
-        nears = []
-        for k in range(SLOTS):
-            off = sign * (cols[k, b] - base - b)
-            picks = []
-            for v in range(VARS):
-                value = window[(REACH - 1) * VARS + v]
-                for d in range(REACH - 1):
-                    value = jnp.where(off == d + 1, window[d * VARS + v], value)
-                picks.append(value if k == 0 else jnp.where(k < counts[side, b], value, 0.0))
-            nears.append([[value] for value in picks])
-        return nears
-
-    def first(b, window):
-        acc = couple(mlow, b, near(window, b, -1, lcols, 0))
-        fresh = tuple(source[b, i] + acc[i][0] for i in range(VARS))
-        return Kept(fresh + window[: STATE - VARS], [(ybuf, (b, i), fresh[i]) for i in range(VARS)])
-
-    steps(blocks, 8, first, entering(0))
-
     def second(e, carry):
         c = blocks - 1 - e
         window, edges = carry[:STATE], list(carry[STATE:])
-        acc = couple(mupp, c, near(window, c, 1, ucols, 1))
+        acc = couple(mupp, c, near_blocks(window, c, base, 1, ucols, counts, 1))
         fresh = tuple(ybuf[c, i] + acc[i][0] for i in range(VARS))
         here = (lane == 2 * c) | (lane == (2 * c + cells - 1) % cells)
         stores = []
@@ -586,14 +581,9 @@
             edges[i] = jnp.where(here, pltpu.roll(fresh[i], 2 * c, 1), edges[i])
         return Kept(fresh + window[: STATE - VARS] + tuple(edges), stores)
 
-    carry = steps(blocks, 8, second, entering(128) + (zero,) * VARS)
+    carry = steps(blocks, 8, second, tuple(start[q] for q in range(STATE)) + (zero,) * VARS)
     for v in range(VARS):
         edge[v] = carry[STATE + v]
-    for m in range(REACH):
-        for v in range(VARS):
-            tail[m, v] = wout[blocks - REACH + m, v]
-    for copy in copies:
-        copy.wait()
 
 
 def inner_kernel(z, w, low, side, lcols, counts, resid, coef, correction, wbuf, sem):
@@ -773,7 +763,7 @@
     tile = (nrhs, cells)
 
     mats = (VARS, VARS, SLOTS, blocks + PAD, cells)
-    padded = (low.shape[0] + PAD, cells)
+    padded = (low.shape[0] + VARS * VARS * SLOTS, cells)
 
     count = half if half <= DIRECT else 1
 
@@ -783,17 +773,18 @@
     def whole(pages):
         return [(half, pages) + tile] if count > 1 else []
 
-    *maps, source, mlow, mupp, lcols, ucols, used = call(
-        functools.partial(parted, functools.partial(local_kernel, half), 7, count, half),
+    *maps, source, mlow, mupp, lcols, ucols, used, low, side = call(
+        functools.partial(parted, functools.partial(local_kernel, half), 8, count, half),
         pieces(parts)
         + [(rhs.shape, VMEM), (mats, VMEM), (mats, VMEM)]
-        + [(lcols.shape, VMEM, jnp.int32)] * 3,
-        (rhs, inv, low, upp, lcols, ucols, used),
-        (HBM,) * 7,
-        [rhs.shape, (VARS, VARS, blocks + PAD, cells), low.shape, upp.shape]
+        + [(lcols.shape, VMEM, jnp.int32)] * 3
+        + [(padded, VMEM)] * 2,
+        (rhs, inv, low, upp, side, lcols, ucols, used),
+        (HBM,) * 8,
+        [rhs.shape, (VARS, VARS, blocks + PAD, cells), padded]
         + [pltpu.SMEM(lcols.shape, jnp.int32)] * 3
         + [(rows, VARS, nrhs + WIDE, cells), (rows, VARS, nrhs + 2 * WIDE, cells)]
-        + [(WIDE * SPACE, cells), pltpu.SemaphoreType.DMA((10,))]
+        + [(WIDE * SPACE + SPACE, cells), pltpu.SemaphoreType.DMA((11,))]
         + whole(parts),
     )
     maps = exchange(maps, half, sides)
@@ -820,19 +811,19 @@
         + whole(back),
     )
     states = exchange(states, half, sides)
-    z, w, tail, edge, low, side = call(
-        functools.partial(joined, functools.partial(sweep_kernel, half), count, half),
-        [
-            (rhs.shape, VMEM),
-            ((blocks + 1, VARS) + tile, VMEM),
-            ((REACH, VARS) + tile, VMEM),
-            ((VARS,) + tile, VMEM),
-            (padded, VMEM),
-            (padded, VMEM),
-        ],
-        (*states, source, mlow, mupp, lcols, ucols, used, low, side),
-        (VMEM,) * (3 + count) + (SMEM,) * 3 + (HBM,) * 2,
-        [rhs.shape, (32 * 8, cells), pltpu.SemaphoreType.DMA((2,))] + whole(back),
+    y, start, tail = call(
+        functools.partial(joined, functools.partial(forward_kernel, half), count, half),
+        [(rhs.shape, VMEM), ((STATE,) + tile, VMEM), ((REACH, VARS) + tile, VMEM)],
+        (*states, source, mlow, mupp, lcols, ucols, used),
+        (VMEM,) * (3 + count) + (SMEM,) * 3,
+        [(33 * 8, cells)] + whole(back),
+    )
+    z, w, edge = call(
+        sweep_kernel,
+        [(rhs.shape, VMEM), ((blocks + 1, VARS) + tile, VMEM), ((VARS,) + tile, VMEM)],
+        (y, start, mupp, ucols, used),
+        (VMEM,) * 3 + (SMEM,) * 2,
+        [],
     )
     tail = lax.ppermute(tail, "chain", [(i, (i + 1) % n) for i in range(n)])
     swap_a, swap_b = (

time: 51.5 us -> 52.1 us (1.012)
  waiting for transfers between devices: 14.4 us -> 12.9 us
  blocking collectives: 9.42 us -> 10.8 us
  Pallas kernels: 13.5 us -> 14.2 us
    ppermute x1, waiting for transfers between devices: 2.86 us -> 1.35 us  [shards(): tail = lax.ppermute(tail, 'chain', [(i, (i + 1) % n) for i in range(n)])]
    all_to_all x1, blocking collectives: 9.42 us -> 10.8 us  [shards(): squares = lax.all_to_all(squares, ('chain', 'sub'), 0, 0, tiled=True)]
    pallas_call x7 -> x8, Pallas kernels: 13.5 us -> 14.2 us  [call(): pl.pallas_call(kernel, out_shape=[jax.ShapeDtypeStruct(o[0], (o + (jnp.fl...]
  transfers between devices with their start and end apart: 10 -> 10, of which waited for: 9 -> 9; matrix products, arithmetic and copies ran while one was open for 0% -> 0% of each run, Pallas kernels for 3% -> 6%
where the time goes in v2:
time: 52.1 us; the launch traced here: 51.9 us
  Pallas kernels  14.2 us (27%)
  starting transfers between devices  13.3 us (26%)
  waiting for transfers between devices  12.9 us (25%)
  blocking collectives  10.8 us (21%)
  between operations  0.69 us (1%)
    pallas_call x8, Pallas kernels, call(): pl.pallas_call(kernel, out_shape=[jax.ShapeDtypeStruct(o[0], (o + (jnp.fl...  14.2 us
    all_to_all x1, blocking collectives, shards(): squares = lax.all_to_all(squares, ('chain', 'sub'), 0, 0, tiled=True)  10.8 us
    ppermute x6, waiting for transfers between devices, exchange(): lax.ppermute(part, 'chain', [(i, i ^ x) for i in range(count)])  8.46 us
    ppermute x6, starting transfers between devices, exchange(): lax.ppermute(part, 'chain', [(i, i ^ x) for i in range(count)])  8.24 us
    ppermute x1, waiting for transfers between devices, shards(): lax.ppermute(offer, 'chain', [p for i in range(half) for p in ((i, i + ha...  2.93 us
    ppermute x1, starting transfers between devices, shards(): lax.ppermute(offer, 'chain', [p for i in range(half) for p in ((i, i + ha...  2.65 us
    ppermute x2, starting transfers between devices, shards(): lax.ppermute(edge, 'sub', [p for i, j in pairs for p in ((i, j), (j, i))])  1.69 us
    ppermute x1, waiting for transfers between devices, shards(): tail = lax.ppermute(tail, 'chain', [(i, (i + 1) % n) for i in range(n)])  1.35 us
  transfers between devices with their start and end apart: 10, of which 9 were waited for; matrix products, arithmetic and copies ran while one was open for 0% of the time, Pallas kernels for 6%

profile of v2, /device:TPU:0, one launch (start us, length us, event | category | flops | bytes accessed | tf_op | source)
XLA Modules:
  0.0 51.9 jit_solution(12334625422559288329)
XLA Ops:
  0.6 6.1 %shard_map.95 = (f32[30,8,128]{2,1,0:T(8,128)S(1)}, f32[30,8,128]{2,1,0:T(8,128)S(1)}, f32[30,8,128]{2,1,0:T(8,128)S(1)}, f32[30,8,128]{2,1,0:T(8,128)S(1)}, f32...) custom-call(f32[24,5,8,128]{3,2,1,0:T(8,128)} %refs_0_.1, ...), custom_call_target="tpu_custom_call" | custom-call | tf_op jit(solution)/shard_map/pallas_call | solution.py:733
  6.8 4.0 %collective-permute-start = (f32[30,8,128]{2,1,0:T(8,128)S(1)}, f32[30,8,128]{2,1,0:T(8,128)S(1)}, u32[]{:S(2)}, u32[]{:S(2)}) collective-permute-start(f32[30,8,128]{2,1,0:T(8,128)S(1)} %get-tuple-element.33), channel_id=1, source_target_pairs={{0,12},{4,8},{8,4},{12,0},{16,28},{20,24},{24,20},{28,16},{1,13},{... | collective-permute-start | bytes 368648 | tf_op jit(solution)/shard_map/ppermute | solution.py:200
  10.8 0.5 collective-permute-start.1
  11.4 3.1 %collective-permute-done.refs_1_ = f32[30,8,128]{2,1,0:T(8,128)S(1)} collective-permute-done((f32[30,8,128]{2,1,0:T(8,128)S(1)}, f32[30,8,128]{2,1,0:T(8,128)S(1)}, u32[]{:S(2)}, u32[]{:S(2)}) %collective-permute-start) | collective-permute-done | bytes 122912 | tf_op jit(solution)/shard_map/ppermute | solution.py:200
  14.5 2.2 %collective-permute-done.1.refs_2_ = f32[30,8,128]{2,1,0:T(8,128)S(1)} collective-permute-done((f32[30,8,128]{2,1,0:T(8,128)S(1)}, f32[30,8,128]{2,1,0:T(8,128)S(1)}, u32[]{:S(2)}, u32[]{:S(2)}) %collective-permute-start.1) | collective-permute-done | bytes 122912 | tf_op jit(solution)/shard_map/ppermute | solution.py:200
  16.9 1.3 %shard_map.96 = (f32[2816,128]{1,0:T(8,128)S(1)}, f32[4,8,8,128]{3,2,1,0:T(8,128)S(1)}, f32[12,8,128]{2,1,0:T(8,128)S(1)}) custom-call(f32[30,8,128]{2,1,0:T(8,128)S(1)} %get-tuple-element.32.refs_0_, f32[30,8,128]{2,1,0:T(8,128)S(1)} %collective-permute-done.refs_1_, f32[30,8,128]{2,1,0:T(8,128)S(1)} %collective-permute-done.1.refs_2_, ...), custom_call_target="tpu_custom_call" | custom-call | tf_op jit(solution)/shard_map/pallas_call | solution.py:733
  18.2 2.7 %collective-permute-start.3 = (f32[12,8,128]{2,1,0:T(8,128)S(1)}, f32[12,8,128]{2,1,0:T(8,128)S(1)}, u32[]{:S(2)}, u32[]{:S(2)}) collective-permute-start(f32[12,8,128]{2,1,0:T(8,128)S(1)} %get-tuple-element.38.refs_2_), channel_id=1, source_target_pairs={{0,16},{16,0},{4,20},{20,4},{8,24},{24,8},{12,28},{28,12},{1,17},{... | collective-permute-start | bytes 147464 | tf_op jit(solution)/shard_map/ppermute | solution.py:802
  20.9 2.9 %collective-permute-done.3.refs_3_ = f32[12,8,128]{2,1,0:T(8,128)S(1)} collective-permute-done((f32[12,8,128]{2,1,0:T(8,128)S(1)}, f32[12,8,128]{2,1,0:T(8,128)S(1)}, u32[]{:S(2)}, u32[]{:S(2)}) %collective-permute-start.3) | collective-permute-done | bytes 49184 | tf_op jit(solution)/shard_map/ppermute | solution.py:802
  23.8 0.3 shard_map.97
  24.1 1.3 %collective-permute-start.4 = (f32[8,8,128]{2,1,0:T(8,128)S(1)}, f32[8,8,128]{2,1,0:T(8,128)S(1)}, u32[]{:S(2)}, u32[]{:S(2)}) collective-permute-start(f32[8,8,128]{2,1,0:T(8,128)S(1)} %get-tuple-element.40), channel_id=1, source_target_pairs={{0,12},{4,8},{8,4},{12,0},{16,28},{20,24},{24,20},{28,16},{1,13},{... | collective-permute-start | bytes 98312 | tf_op jit(solution)/shard_map/ppermute | solution.py:200
  25.4 1.3 %collective-permute-start.5 = (f32[8,8,128]{2,1,0:T(8,128)S(1)}, f32[8,8,128]{2,1,0:T(8,128)S(1)}, u32[]{:S(2)}, u32[]{:S(2)}) collective-permute-start(f32[8,8,128]{2,1,0:T(8,128)S(1)} %get-tuple-element.41), channel_id=1, source_target_pairs={{0,4},{4,0},{8,12},{12,8},{16,20},{20,16},{24,28},{28,24},{1,5},{5... | collective-permute-start | bytes 98312 | tf_op jit(solution)/shard_map/ppermute | solution.py:200
  26.7 0.9 %collective-permute-start.6 = (f32[8,8,128]{2,1,0:T(8,128)S(1)}, f32[8,8,128]{2,1,0:T(8,128)S(1)}, u32[]{:S(2)}, u32[]{:S(2)}) collective-permute-start(f32[8,8,128]{2,1,0:T(8,128)S(1)} %get-tuple-element.42), channel_id=1, source_target_pairs={{0,8},{4,12},{8,0},{12,4},{16,24},{20,28},{24,16},{28,20},{1,9},{5... | collective-permute-start | bytes 98312 | tf_op jit(solution)/shard_map/ppermute | solution.py:200
  27.6 1.3 %collective-permute-done.4.refs_1_ = f32[8,8,128]{2,1,0:T(8,128)S(1)} collective-permute-done((f32[8,8,128]{2,1,0:T(8,128)S(1)}, f32[8,8,128]{2,1,0:T(8,128)S(1)}, u32[]{:S(2)}, u32[]{:S(2)}) %collective-permute-start.4) | collective-permute-done | bytes 32800 | tf_op jit(solution)/shard_map/ppermute | solution.py:200
  29.0 0.4 collective-permute-done.5.refs_2_
  29.3 1.3 %collective-permute-done.6.refs_3_ = f32[8,8,128]{2,1,0:T(8,128)S(1)} collective-permute-done((f32[8,8,128]{2,1,0:T(8,128)S(1)}, f32[8,8,128]{2,1,0:T(8,128)S(1)}, u32[]{:S(2)}, u32[]{:S(2)}) %collective-permute-start.6) | collective-permute-done | bytes 32800 | tf_op jit(solution)/shard_map/ppermute | solution.py:200
  30.6 1.4 %shard_map.98 = (f32[24,5,8,128]{3,2,1,0:T(8,128)S(1)}, f32[15,8,128]{2,1,0:T(8,128)S(1)}, f32[3,5,8,128]{3,2,1,0:T(8,128)S(1)}) custom-call(f32[8,8,128]{2,1,0:T(8,128)S(1)} %get-tuple-element.39.refs_0_, f32[8,8,128]{2,1,0:T(8,128)S(1)} %collective-permute-done.4.refs_1_, f32[8,8,128]{2,1,0:T(8,128)S(1)} %collective-permute-done.5.refs_2_, ...), custom_call_target="tpu_custom_call" | custom-call | tf_op jit(solution)/shard_map/pallas_call | solution.py:733
  32.1 0.8 %collective-permute-start.7 = (f32[3,5,8,128]{3,2,1,0:T(8,128)S(1)}, f32[3,5,8,128]{3,2,1,0:T(8,128)S(1)}, u32[]{:S(2)}, u32[]{:S(2)}) collective-permute-start(f32[3,5,8,128]{3,2,1,0:T(8,128)S(1)} %get-tuple-element.58), channel_id=1, source_target_pairs={{0,4},{4,8},{8,12},{12,16},{16,20},{20,24},{24,28},{28,0},{1,5},{5... | collective-permute-start | bytes 184328 | tf_op jit(solution)/shard_map/ppermute | solution.py:828
  32.8 1.5 %shard_map.99 = (f32[24,5,8,128]{3,2,1,0:T(8,128)S(1)}, f32[25,5,8,128]{3,2,1,0:T(8,128)S(1)}, f32[5,8,128]{2,1,0:T(8,128)S(1)}) custom-call(f32[24,5,8,128]{3,2,1,0:T(8,128)S(1)} %get-tuple-element.49.ybuf, f32[15,8,128]{2,1,0:T(8,128)S(1)} %get-tuple-element.50.start, f32[5,5,2,32,128]{4,3,2,1,0:T(8,128)S(1)} %get-tuple-element.45.refs_6_.mupp, ...), custom_call_target="tpu_custom_call" | custom-call | tf_op jit(solution)/shard_map/pallas_call | solution.py:733
  34.4 1.6 %collective-permute-start.8 = (f32[5,8,128]{2,1,0:T(8,128)S(1)}, f32[5,8,128]{2,1,0:T(8,128)S(1)}, u32[]{:S(2)}, u32[]{:S(2)}) collective-permute-start(f32[5,8,128]{2,1,0:T(8,128)S(1)} %get-tuple-element.59), channel_id=1, source_target_pairs={{0,1},{1,0},{2,3},{3,2},{4,5},{5,4},{6,7},{7,6},{8,9},{9,8},{10,11... | collective-permute-start | bytes 61448 | tf_op jit(solution)/shard_map/ppermute | solution.py:830
  36.0 1.5 %shard_map.100 = (f32[24,5,8,128]{3,2,1,0:T(8,128)S(1)}, f32[7,8,128]{2,1,0:T(8,128)S(1)}, f32[24,5,8,128]{3,2,1,0:T(8,128)}) custom-call(f32[24,5,8,128]{3,2,1,0:T(8,128)S(1)} %get-tuple-element.51.z, f32[25,5,8,128]{3,2,1,0:T(8,128)S(1)} %get-tuple-element.52.w, f32[1250,128]{1,0:T(8,128)S(1)} %get-tuple-element.53.low, ...), custom_call_target="tpu_custom_call" | custom-call | tf_op jit(solution)/shard_map/pallas_call | solution.py:733
  37.7 1.4 %collective-permute-done.7.tail = f32[3,5,8,128]{3,2,1,0:T(8,128)S(1)} collective-permute-done((f32[3,5,8,128]{3,2,1,0:T(8,128)S(1)}, f32[3,5,8,128]{3,2,1,0:T(8,128)S(1)}, u32[]{:S(2)}, u32[]{:S(2)}) %collective-permute-start.7) | collective-permute-done | bytes 61472 | tf_op jit(solution)/shard_map/ppermute | solution.py:828
  39.0 1.1 %shard_map.101 = (f32[24,5,8,128]{3,2,1,0:T(8,128)S(1)}, f32[32,1,128]{2,1,0:T(1,128)S(1)}) custom-call(f32[24,5,8,128]{3,2,1,0:T(8,128)S(1)} %get-tuple-element.56.inner, f32[7,8,128]{2,1,0:T(8,128)S(1)} %get-tuple-element.57.coef, f32[1250,128]{1,0:T(8,128)S(1)} %get-tuple-element.53.low, f32[3,5,8,128]{3,2,1,0:T(8,128)S(1)} %collective-permute-done.7.tail, ...), custom_call_target="tpu_custom_call" | custom-call | tf_op jit(solution)/shard_map/pallas_call | solution.py:733
  40.2 10.8 %all_to_all.5.squares = f32[32,1,128]{2,1,0:T(1,128)S(1)} all-to-all(f32[32,1,128]{2,1,0:T(1,128)S(1)} %get-tuple-element.61), channel_id=1, replica_groups=mesh['chain'=8,'sub'=4] {'chain','sub'}, dimensions={0} | all-to-all | bytes 32768 | tf_op jit(solution)/shard_map/all_to_all | solution.py:854
  51.0 0.9 %shard_map.102 = f32[24,5,8,128]{3,2,1,0:T(8,128)} custom-call(f32[24,5,8,128]{3,2,1,0:T(8,128)S(1)} %get-tuple-element.60.resid, f32[32,1,128]{2,1,0:T(1,128)S(1)} %all_to_all.5.squares), custom_call_target="tpu_custom_call" | custom-call | tf_op jit(solution)/shard_map/pallas_call | solution.py:733
  (5 shorter events, 0.5 us)
Async XLA Ops:
  6.8 7.8 %collective-permute-start = (f32[30,8,128]{2,1,0:T(8,128)S(1)}, f32[30,8,128]{2,1,0:T(8,128)S(1)}, u32[]{:S(2)}, u32[]{:S(2)}) collective-permute-start(f32[30,8,128]{2,1,0:T(8,128)S(1)} %get-tuple-element.33), channel_id=1, source_target_pairs={{0,12},{4,8},{8,4},{12,0},{16,28},{20,24},{24,20},{28,16},{1,13},{... | collective-permute-start | bytes 368648 | tf_op jit(solution)/shard_map/ppermute | solution.py:200
  10.8 6.0 %collective-permute-start.1 = (f32[30,8,128]{2,1,0:T(8,128)S(1)}, f32[30,8,128]{2,1,0:T(8,128)S(1)}, u32[]{:S(2)}, u32[]{:S(2)}) collective-permute-start(f32[30,8,128]{2,1,0:T(8,128)S(1)} %get-tuple-element.34), channel_id=1, source_target_pairs={{0,4},{4,0},{8,12},{12,8},{16,20},{20,16},{24,28},{28,24},{1,5},{5... | collective-permute-start | bytes 368648 | tf_op jit(solution)/shard_map/ppermute | solution.py:200
  11.3 5.6 %collective-permute-start.2 = (f32[30,8,128]{2,1,0:T(8,128)S(1)}, f32[30,8,128]{2,1,0:T(8,128)S(1)}, u32[]{:S(2)}, u32[]{:S(2)}) collective-permute-start(f32[30,8,128]{2,1,0:T(8,128)S(1)} %get-tuple-element.35), channel_id=1, source_target_pairs={{0,8},{4,12},{8,0},{12,4},{16,24},{20,28},{24,16},{28,20},{1,9},{5... | collective-permute-start | bytes 368648 | tf_op jit(solution)/shard_map/ppermute | solution.py:200
  18.2 5.6 %collective-permute-start.3 = (f32[12,8,128]{2,1,0:T(8,128)S(1)}, f32[12,8,128]{2,1,0:T(8,128)S(1)}, u32[]{:S(2)}, u32[]{:S(2)}) collective-permute-start(f32[12,8,128]{2,1,0:T(8,128)S(1)} %get-tuple-element.38.refs_2_), channel_id=1, source_target_pairs={{0,16},{16,0},{4,20},{20,4},{8,24},{24,8},{12,28},{28,12},{1,17},{... | collective-permute-start | bytes 147464 | tf_op jit(solution)/shard_map/ppermute | solution.py:802
  24.1 4.9 %collective-permute-start.4 = (f32[8,8,128]{2,1,0:T(8,128)S(1)}, f32[8,8,128]{2,1,0:T(8,128)S(1)}, u32[]{:S(2)}, u32[]{:S(2)}) collective-permute-start(f32[8,8,128]{2,1,0:T(8,128)S(1)} %get-tuple-element.40), channel_id=1, source_target_pairs={{0,12},{4,8},{8,4},{12,0},{16,28},{20,24},{24,20},{28,16},{1,13},{... | collective-permute-start | bytes 98312 | tf_op jit(solution)/shard_map/ppermute | solution.py:200
  25.4 3.9 %collective-permute-start.5 = (f32[8,8,128]{2,1,0:T(8,128)S(1)}, f32[8,8,128]{2,1,0:T(8,128)S(1)}, u32[]{:S(2)}, u32[]{:S(2)}) collective-permute-start(f32[8,8,128]{2,1,0:T(8,128)S(1)} %get-tuple-element.41), channel_id=1, source_target_pairs={{0,4},{4,0},{8,12},{12,8},{16,20},{20,16},{24,28},{28,24},{1,5},{5... | collective-permute-start | bytes 98312 | tf_op jit(solution)/shard_map/ppermute | solution.py:200
  26.7 3.9 %collective-permute-start.6 = (f32[8,8,128]{2,1,0:T(8,128)S(1)}, f32[8,8,128]{2,1,0:T(8,128)S(1)}, u32[]{:S(2)}, u32[]{:S(2)}) collective-permute-start(f32[8,8,128]{2,1,0:T(8,128)S(1)} %get-tuple-element.42), channel_id=1, source_target_pairs={{0,8},{4,12},{8,0},{12,4},{16,24},{20,28},{24,16},{28,20},{1,9},{5... | collective-permute-start | bytes 98312 | tf_op jit(solution)/shard_map/ppermute | solution.py:200
  32.1 7.0 %collective-permute-start.7 = (f32[3,5,8,128]{3,2,1,0:T(8,128)S(1)}, f32[3,5,8,128]{3,2,1,0:T(8,128)S(1)}, u32[]{:S(2)}, u32[]{:S(2)}) collective-permute-start(f32[3,5,8,128]{3,2,1,0:T(8,128)S(1)} %get-tuple-element.58), channel_id=1, source_target_pairs={{0,4},{4,8},{8,12},{12,16},{16,20},{20,24},{24,28},{28,0},{1,5},{5... | collective-permute-start | bytes 184328 | tf_op jit(solution)/shard_map/ppermute | solution.py:828
  34.3 3.4 %collective-permute-start.9 = (f32[5,8,128]{2,1,0:T(8,128)S(1)}, f32[5,8,128]{2,1,0:T(8,128)S(1)}, u32[]{:S(2)}, u32[]{:S(2)}) collective-permute-start(f32[5,8,128]{2,1,0:T(8,128)S(1)} %get-tuple-element.59), channel_id=1, source_target_pairs={{1,2},{2,1},{0,3},{3,0},{5,6},{6,5},{4,7},{7,4},{9,10},{10,9},{8,1... | collective-permute-start | bytes 61448 | tf_op jit(solution)/shard_map/ppermute | solution.py:830
  34.4 3.3 %collective-permute-start.8 = (f32[5,8,128]{2,1,0:T(8,128)S(1)}, f32[5,8,128]{2,1,0:T(8,128)S(1)}, u32[]{:S(2)}, u32[]{:S(2)}) collective-permute-start(f32[5,8,128]{2,1,0:T(8,128)S(1)} %get-tuple-element.59), channel_id=1, source_target_pairs={{0,1},{1,0},{2,3},{3,2},{4,5},{5,4},{6,7},{7,6},{8,9},{9,8},{10,11... | collective-permute-start | bytes 61448 | tf_op jit(solution)/shard_map/ppermute | solution.py:830

commit v3 on v1

--- a/solution.py
+++ b/solution.py
@@ -235,12 +235,12 @@
         for k, (src, dst) in enumerate(
             (
                 (inv_h, inv.at[:, :, pl.ds(0, rhs.shape[0]), :]),
-                (low_h, low),
+                (low_h, low.at[pl.ds(0, low_h.shape[0]), :]),
                 (lcols_h, lcols),
                 (counts_h, counts),
                 (ucols_h, ucols),
                 (rhs_h, rhs),
-                (upp_h, upp),
+                (upp_h, upp.at[pl.ds(0, upp_h.shape[0]), :]),
                 (lcols_h, lcols_v),
                 (ucols_h, ucols_v),
                 (counts_h, counts_v),
@@ -572,7 +572,7 @@
         fresh = tuple(source[b, i] + acc[i][0] for i in range(VARS))
         return Kept(fresh + window[: STATE - VARS], [(ybuf, (b, i), fresh[i]) for i in range(VARS)])
 
-    steps(blocks, 8, first, entering(0))
+    steps(blocks, 12, first, entering(0))
 
     def second(e, carry):
         c = blocks - 1 - e
@@ -586,7 +586,7 @@
             edges[i] = jnp.where(here, pltpu.roll(fresh[i], 2 * c, 1), edges[i])
         return Kept(fresh + window[: STATE - VARS] + tuple(edges), stores)
 
-    carry = steps(blocks, 8, second, entering(128) + (zero,) * VARS)
+    carry = steps(blocks, 12, second, entering(128) + (zero,) * VARS)
     for v in range(VARS):
         edge[v] = carry[STATE + v]
     for m in range(REACH):
@@ -773,7 +773,7 @@
     tile = (nrhs, cells)
 
     mats = (VARS, VARS, SLOTS, blocks + PAD, cells)
-    padded = (low.shape[0] + PAD, cells)
+    padded = (low.shape[0] + VARS * VARS * SLOTS, cells)
 
     count = half if half <= DIRECT else 1
 
@@ -790,10 +790,10 @@
         + [(lcols.shape, VMEM, jnp.int32)] * 3,
         (rhs, inv, low, upp, lcols, ucols, used),
         (HBM,) * 7,
-        [rhs.shape, (VARS, VARS, blocks + PAD, cells), low.shape, upp.shape]
+        [rhs.shape, (VARS, VARS, blocks + PAD, cells), padded, padded]
         + [pltpu.SMEM(lcols.shape, jnp.int32)] * 3
         + [(rows, VARS, nrhs + WIDE, cells), (rows, VARS, nrhs + 2 * WIDE, cells)]
-        + [(WIDE * SPACE, cells), pltpu.SemaphoreType.DMA((10,))]
+        + [(WIDE * SPACE + SPACE, cells), pltpu.SemaphoreType.DMA((10,))]
         + whole(parts),
     )
     maps = exchange(maps, half, sides)
@@ -832,7 +832,7 @@
         ],
         (*states, source, mlow, mupp, lcols, ucols, used, low, side),
         (VMEM,) * (3 + count) + (SMEM,) * 3 + (HBM,) * 2,
-        [rhs.shape, (32 * 8, cells), pltpu.SemaphoreType.DMA((2,))] + whole(back),
+        [rhs.shape, (33 * 8, cells), pltpu.SemaphoreType.DMA((2,))] + whole(back),
     )
     tail = lax.ppermute(tail, "chain", [(i, (i + 1) % n) for i in range(n)])
     swap_a, swap_b = (

time: 51.5 us -> 51.4 us (level)
  no operation moved by 1% of the time
where the time goes in v3:
time: 51.4 us; the launch traced here: 51.2 us
  waiting for transfers between devices  14.4 us (28%)
  Pallas kernels  13.4 us (26%)
  starting transfers between devices  13.3 us (26%)
  blocking collectives  9.41 us (18%)
  between operations  0.69 us (1%)
    pallas_call x7, Pallas kernels, call(): pl.pallas_call(kernel, out_shape=[jax.ShapeDtypeStruct(o[0], (o + (jnp.fl...  13.4 us
    all_to_all x1, blocking collectives, shards(): squares = lax.all_to_all(squares, ('chain', 'sub'), 0, 0, tiled=True)  9.41 us
    ppermute x6, waiting for transfers between devices, exchange(): lax.ppermute(part, 'chain', [(i, i ^ x) for i in range(count)])  8.46 us
    ppermute x6, starting transfers between devices, exchange(): lax.ppermute(part, 'chain', [(i, i ^ x) for i in range(count)])  8.25 us
    ppermute x1, waiting for transfers between devices, shards(): lax.ppermute(offer, 'chain', [p for i in range(half) for p in ((i, i + ha...  2.92 us
    ppermute x1, waiting for transfers between devices, shards(): tail = lax.ppermute(tail, 'chain', [(i, (i + 1) % n) for i in range(n)])  2.85 us
    ppermute x1, starting transfers between devices, shards(): lax.ppermute(offer, 'chain', [p for i in range(half) for p in ((i, i + ha...  2.66 us
    ppermute x2, starting transfers between devices, shards(): lax.ppermute(edge, 'sub', [p for i, j in pairs for p in ((i, j), (j, i))])  1.63 us
  transfers between devices with their start and end apart: 10, of which 9 were waited for; matrix products, arithmetic and copies ran while one was open for 0% of the time, Pallas kernels for 3%

profile of v3, /device:TPU:0, one launch (start us, length us, event | category | flops | bytes accessed | tf_op | source)
XLA Modules:
  0.0 51.2 jit_solution(6133848296461310275)
XLA Ops:
  0.6 6.0 %shard_map.95 = (f32[30,8,128]{2,1,0:T(8,128)S(1)}, f32[30,8,128]{2,1,0:T(8,128)S(1)}, f32[30,8,128]{2,1,0:T(8,128)S(1)}, f32[30,8,128]{2,1,0:T(8,128)S(1)}, f32...) custom-call(f32[24,5,8,128]{3,2,1,0:T(8,128)} %refs_0_.1, ...), custom_call_target="tpu_custom_call" | custom-call | tf_op jit(solution)/shard_map/pallas_call | solution.py:743
  6.6 4.1 %collective-permute-start = (f32[30,8,128]{2,1,0:T(8,128)S(1)}, f32[30,8,128]{2,1,0:T(8,128)S(1)}, u32[]{:S(2)}, u32[]{:S(2)}) collective-permute-start(f32[30,8,128]{2,1,0:T(8,128)S(1)} %get-tuple-element.31), channel_id=1, source_target_pairs={{0,12},{4,8},{8,4},{12,0},{16,28},{20,24},{24,20},{28,16},{1,13},{... | collective-permute-start | bytes 368648 | tf_op jit(solution)/shard_map/ppermute | solution.py:200
  10.7 0.5 collective-permute-start.1
  11.3 3.1 %collective-permute-done.refs_1_ = f32[30,8,128]{2,1,0:T(8,128)S(1)} collective-permute-done((f32[30,8,128]{2,1,0:T(8,128)S(1)}, f32[30,8,128]{2,1,0:T(8,128)S(1)}, u32[]{:S(2)}, u32[]{:S(2)}) %collective-permute-start) | collective-permute-done | bytes 122912 | tf_op jit(solution)/shard_map/ppermute | solution.py:200
  14.4 2.2 %collective-permute-done.1.refs_2_ = f32[30,8,128]{2,1,0:T(8,128)S(1)} collective-permute-done((f32[30,8,128]{2,1,0:T(8,128)S(1)}, f32[30,8,128]{2,1,0:T(8,128)S(1)}, u32[]{:S(2)}, u32[]{:S(2)}) %collective-permute-start.1) | collective-permute-done | bytes 122912 | tf_op jit(solution)/shard_map/ppermute | solution.py:200
  16.8 1.3 %shard_map.96 = (f32[2816,128]{1,0:T(8,128)S(1)}, f32[4,8,8,128]{3,2,1,0:T(8,128)S(1)}, f32[12,8,128]{2,1,0:T(8,128)S(1)}) custom-call(f32[30,8,128]{2,1,0:T(8,128)S(1)} %get-tuple-element.30.refs_0_, f32[30,8,128]{2,1,0:T(8,128)S(1)} %collective-permute-done.refs_1_, f32[30,8,128]{2,1,0:T(8,128)S(1)} %collective-permute-done.1.refs_2_, ...), custom_call_target="tpu_custom_call" | custom-call | tf_op jit(solution)/shard_map/pallas_call | solution.py:743
  18.1 2.7 %collective-permute-start.3 = (f32[12,8,128]{2,1,0:T(8,128)S(1)}, f32[12,8,128]{2,1,0:T(8,128)S(1)}, u32[]{:S(2)}, u32[]{:S(2)}) collective-permute-start(f32[12,8,128]{2,1,0:T(8,128)S(1)} %get-tuple-element.36.refs_2_), channel_id=1, source_target_pairs={{0,16},{16,0},{4,20},{20,4},{8,24},{24,8},{12,28},{28,12},{1,17},{... | collective-permute-start | bytes 147464 | tf_op jit(solution)/shard_map/ppermute | solution.py:811
  20.8 2.9 %collective-permute-done.3.refs_3_ = f32[12,8,128]{2,1,0:T(8,128)S(1)} collective-permute-done((f32[12,8,128]{2,1,0:T(8,128)S(1)}, f32[12,8,128]{2,1,0:T(8,128)S(1)}, u32[]{:S(2)}, u32[]{:S(2)}) %collective-permute-start.3) | collective-permute-done | bytes 49184 | tf_op jit(solution)/shard_map/ppermute | solution.py:811
  23.7 0.3 shard_map.97
  24.0 1.3 %collective-permute-start.4 = (f32[8,8,128]{2,1,0:T(8,128)S(1)}, f32[8,8,128]{2,1,0:T(8,128)S(1)}, u32[]{:S(2)}, u32[]{:S(2)}) collective-permute-start(f32[8,8,128]{2,1,0:T(8,128)S(1)} %get-tuple-element.38), channel_id=1, source_target_pairs={{0,12},{4,8},{8,4},{12,0},{16,28},{20,24},{24,20},{28,16},{1,13},{... | collective-permute-start | bytes 98312 | tf_op jit(solution)/shard_map/ppermute | solution.py:200
  25.3 1.3 %collective-permute-start.5 = (f32[8,8,128]{2,1,0:T(8,128)S(1)}, f32[8,8,128]{2,1,0:T(8,128)S(1)}, u32[]{:S(2)}, u32[]{:S(2)}) collective-permute-start(f32[8,8,128]{2,1,0:T(8,128)S(1)} %get-tuple-element.39), channel_id=1, source_target_pairs={{0,4},{4,0},{8,12},{12,8},{16,20},{20,16},{24,28},{28,24},{1,5},{5... | collective-permute-start | bytes 98312 | tf_op jit(solution)/shard_map/ppermute | solution.py:200
  26.6 0.9 %collective-permute-start.6 = (f32[8,8,128]{2,1,0:T(8,128)S(1)}, f32[8,8,128]{2,1,0:T(8,128)S(1)}, u32[]{:S(2)}, u32[]{:S(2)}) collective-permute-start(f32[8,8,128]{2,1,0:T(8,128)S(1)} %get-tuple-element.40), channel_id=1, source_target_pairs={{0,8},{4,12},{8,0},{12,4},{16,24},{20,28},{24,16},{28,20},{1,9},{5... | collective-permute-start | bytes 98312 | tf_op jit(solution)/shard_map/ppermute | solution.py:200
  27.5 1.3 %collective-permute-done.4.refs_1_ = f32[8,8,128]{2,1,0:T(8,128)S(1)} collective-permute-done((f32[8,8,128]{2,1,0:T(8,128)S(1)}, f32[8,8,128]{2,1,0:T(8,128)S(1)}, u32[]{:S(2)}, u32[]{:S(2)}) %collective-permute-start.4) | collective-permute-done | bytes 32800 | tf_op jit(solution)/shard_map/ppermute | solution.py:200
  28.9 0.4 collective-permute-done.5.refs_2_
  29.2 1.3 %collective-permute-done.6.refs_3_ = f32[8,8,128]{2,1,0:T(8,128)S(1)} collective-permute-done((f32[8,8,128]{2,1,0:T(8,128)S(1)}, f32[8,8,128]{2,1,0:T(8,128)S(1)}, u32[]{:S(2)}, u32[]{:S(2)}) %collective-permute-start.6) | collective-permute-done | bytes 32800 | tf_op jit(solution)/shard_map/ppermute | solution.py:200
  30.5 2.2 %shard_map.98 = (f32[24,5,8,128]{3,2,1,0:T(8,128)S(1)}, f32[25,5,8,128]{3,2,1,0:T(8,128)S(1)}, f32[3,5,8,128]{3,2,1,0:T(8,128)S(1)}, f32[5,8,128]{2,1,0:T(8,128)...) custom-call(f32[8,8,128]{2,1,0:T(8,128)S(1)} %get-tuple-element.37.refs_0_, ...), custom_call_target="tpu_custom_call" | custom-call | tf_op jit(solution)/shard_map/pallas_call | solution.py:743
  32.7 0.8 %collective-permute-start.7 = (f32[3,5,8,128]{3,2,1,0:T(8,128)S(1)}, f32[3,5,8,128]{3,2,1,0:T(8,128)S(1)}, u32[]{:S(2)}, u32[]{:S(2)}) collective-permute-start(f32[3,5,8,128]{3,2,1,0:T(8,128)S(1)} %get-tuple-element.54), channel_id=1, source_target_pairs={{0,4},{4,8},{8,12},{12,16},{16,20},{20,24},{24,28},{28,0},{1,5},{5... | collective-permute-start | bytes 184328 | tf_op jit(solution)/shard_map/ppermute | solution.py:837
  33.5 1.6 %collective-permute-start.8 = (f32[5,8,128]{2,1,0:T(8,128)S(1)}, f32[5,8,128]{2,1,0:T(8,128)S(1)}, u32[]{:S(2)}, u32[]{:S(2)}) collective-permute-start(f32[5,8,128]{2,1,0:T(8,128)S(1)} %get-tuple-element.55), channel_id=1, source_target_pairs={{0,1},{1,0},{2,3},{3,2},{4,5},{5,4},{6,7},{7,6},{8,9},{9,8},{10,11... | collective-permute-start | bytes 61448 | tf_op jit(solution)/shard_map/ppermute | solution.py:839
  35.1 1.5 %shard_map.99 = (f32[24,5,8,128]{3,2,1,0:T(8,128)S(1)}, f32[7,8,128]{2,1,0:T(8,128)S(1)}, f32[24,5,8,128]{3,2,1,0:T(8,128)}) custom-call(f32[24,5,8,128]{3,2,1,0:T(8,128)S(1)} %get-tuple-element.47.z, f32[25,5,8,128]{3,2,1,0:T(8,128)S(1)} %get-tuple-element.48.w, f32[1250,128]{1,0:T(8,128)S(1)} %get-tuple-element.49.low, ...), custom_call_target="tpu_custom_call" | custom-call | tf_op jit(solution)/shard_map/pallas_call | solution.py:743
  36.6 0.2 collective-permute-done.9.swap_b
  36.9 2.9 %collective-permute-done.7.tail = f32[3,5,8,128]{3,2,1,0:T(8,128)S(1)} collective-permute-done((f32[3,5,8,128]{3,2,1,0:T(8,128)S(1)}, f32[3,5,8,128]{3,2,1,0:T(8,128)S(1)}, u32[]{:S(2)}, u32[]{:S(2)}) %collective-permute-start.7) | collective-permute-done | bytes 61472 | tf_op jit(solution)/shard_map/ppermute | solution.py:837
  39.7 1.1 %shard_map.100 = (f32[24,5,8,128]{3,2,1,0:T(8,128)S(1)}, f32[32,1,128]{2,1,0:T(1,128)S(1)}) custom-call(f32[24,5,8,128]{3,2,1,0:T(8,128)S(1)} %get-tuple-element.52.inner, f32[7,8,128]{2,1,0:T(8,128)S(1)} %get-tuple-element.53.coef, f32[1250,128]{1,0:T(8,128)S(1)} %get-tuple-element.49.low, f32[3,5,8,128]{3,2,1,0:T(8,128)S(1)} %collective-permute-done.7.tail, ...), custom_call_target="tpu_custom_call" | custom-call | tf_op jit(solution)/shard_map/pallas_call | solution.py:743
  40.9 9.4 %all_to_all.5.squares = f32[32,1,128]{2,1,0:T(1,128)S(1)} all-to-all(f32[32,1,128]{2,1,0:T(1,128)S(1)} %get-tuple-element.57), channel_id=1, replica_groups=mesh['chain'=8,'sub'=4] {'chain','sub'}, dimensions={0} | all-to-all | bytes 32768 | tf_op jit(solution)/shard_map/all_to_all | solution.py:863
  50.3 0.9 %shard_map.101 = f32[24,5,8,128]{3,2,1,0:T(8,128)} custom-call(f32[24,5,8,128]{3,2,1,0:T(8,128)S(1)} %get-tuple-element.56.resid, f32[32,1,128]{2,1,0:T(1,128)S(1)} %all_to_all.5.squares), custom_call_target="tpu_custom_call" | custom-call | tf_op jit(solution)/shard_map/pallas_call | solution.py:743
  (4 shorter events, 0.3 us)
Async XLA Ops:
  6.6 7.8 %collective-permute-start = (f32[30,8,128]{2,1,0:T(8,128)S(1)}, f32[30,8,128]{2,1,0:T(8,128)S(1)}, u32[]{:S(2)}, u32[]{:S(2)}) collective-permute-start(f32[30,8,128]{2,1,0:T(8,128)S(1)} %get-tuple-element.31), channel_id=1, source_target_pairs={{0,12},{4,8},{8,4},{12,0},{16,28},{20,24},{24,20},{28,16},{1,13},{... | collective-permute-start | bytes 368648 | tf_op jit(solution)/shard_map/ppermute | solution.py:200
  10.7 6.0 %collective-permute-start.1 = (f32[30,8,128]{2,1,0:T(8,128)S(1)}, f32[30,8,128]{2,1,0:T(8,128)S(1)}, u32[]{:S(2)}, u32[]{:S(2)}) collective-permute-start(f32[30,8,128]{2,1,0:T(8,128)S(1)} %get-tuple-element.32), channel_id=1, source_target_pairs={{0,4},{4,0},{8,12},{12,8},{16,20},{20,16},{24,28},{28,24},{1,5},{5... | collective-permute-start | bytes 368648 | tf_op jit(solution)/shard_map/ppermute | solution.py:200
  11.2 5.6 %collective-permute-start.2 = (f32[30,8,128]{2,1,0:T(8,128)S(1)}, f32[30,8,128]{2,1,0:T(8,128)S(1)}, u32[]{:S(2)}, u32[]{:S(2)}) collective-permute-start(f32[30,8,128]{2,1,0:T(8,128)S(1)} %get-tuple-element.33), channel_id=1, source_target_pairs={{0,8},{4,12},{8,0},{12,4},{16,24},{20,28},{24,16},{28,20},{1,9},{5... | collective-permute-start | bytes 368648 | tf_op jit(solution)/shard_map/ppermute | solution.py:200
  18.1 5.6 %collective-permute-start.3 = (f32[12,8,128]{2,1,0:T(8,128)S(1)}, f32[12,8,128]{2,1,0:T(8,128)S(1)}, u32[]{:S(2)}, u32[]{:S(2)}) collective-permute-start(f32[12,8,128]{2,1,0:T(8,128)S(1)} %get-tuple-element.36.refs_2_), channel_id=1, source_target_pairs={{0,16},{16,0},{4,20},{20,4},{8,24},{24,8},{12,28},{28,12},{1,17},{... | collective-permute-start | bytes 147464 | tf_op jit(solution)/shard_map/ppermute | solution.py:811
  24.0 4.9 %collective-permute-start.4 = (f32[8,8,128]{2,1,0:T(8,128)S(1)}, f32[8,8,128]{2,1,0:T(8,128)S(1)}, u32[]{:S(2)}, u32[]{:S(2)}) collective-permute-start(f32[8,8,128]{2,1,0:T(8,128)S(1)} %get-tuple-element.38), channel_id=1, source_target_pairs={{0,12},{4,8},{8,4},{12,0},{16,28},{20,24},{24,20},{28,16},{1,13},{... | collective-permute-start | bytes 98312 | tf_op jit(solution)/shard_map/ppermute | solution.py:200
  25.3 3.9 %collective-permute-start.5 = (f32[8,8,128]{2,1,0:T(8,128)S(1)}, f32[8,8,128]{2,1,0:T(8,128)S(1)}, u32[]{:S(2)}, u32[]{:S(2)}) collective-permute-start(f32[8,8,128]{2,1,0:T(8,128)S(1)} %get-tuple-element.39), channel_id=1, source_target_pairs={{0,4},{4,0},{8,12},{12,8},{16,20},{20,16},{24,28},{28,24},{1,5},{5... | collective-permute-start | bytes 98312 | tf_op jit(solution)/shard_map/ppermute | solution.py:200
  26.6 3.9 %collective-permute-start.6 = (f32[8,8,128]{2,1,0:T(8,128)S(1)}, f32[8,8,128]{2,1,0:T(8,128)S(1)}, u32[]{:S(2)}, u32[]{:S(2)}) collective-permute-start(f32[8,8,128]{2,1,0:T(8,128)S(1)} %get-tuple-element.40), channel_id=1, source_target_pairs={{0,8},{4,12},{8,0},{12,4},{16,24},{20,28},{24,16},{28,20},{1,9},{5... | collective-permute-start | bytes 98312 | tf_op jit(solution)/shard_map/ppermute | solution.py:200
  32.7 7.0 %collective-permute-start.7 = (f32[3,5,8,128]{3,2,1,0:T(8,128)S(1)}, f32[3,5,8,128]{3,2,1,0:T(8,128)S(1)}, u32[]{:S(2)}, u32[]{:S(2)}) collective-permute-start(f32[3,5,8,128]{3,2,1,0:T(8,128)S(1)} %get-tuple-element.54), channel_id=1, source_target_pairs={{0,4},{4,8},{8,12},{12,16},{16,20},{20,24},{24,28},{28,0},{1,5},{5... | collective-permute-start | bytes 184328 | tf_op jit(solution)/shard_map/ppermute | solution.py:837
  33.5 3.4 %collective-permute-start.9 = (f32[5,8,128]{2,1,0:T(8,128)S(1)}, f32[5,8,128]{2,1,0:T(8,128)S(1)}, u32[]{:S(2)}, u32[]{:S(2)}) collective-permute-start(f32[5,8,128]{2,1,0:T(8,128)S(1)} %get-tuple-element.55), channel_id=1, source_target_pairs={{1,2},{2,1},{0,3},{3,0},{5,6},{6,5},{4,7},{7,4},{9,10},{10,9},{8,1... | collective-permute-start | bytes 61448 | tf_op jit(solution)/shard_map/ppermute | solution.py:839
  33.5 3.4 %collective-permute-start.8 = (f32[5,8,128]{2,1,0:T(8,128)S(1)}, f32[5,8,128]{2,1,0:T(8,128)S(1)}, u32[]{:S(2)}, u32[]{:S(2)}) collective-permute-start(f32[5,8,128]{2,1,0:T(8,128)S(1)} %get-tuple-element.55), channel_id=1, source_target_pairs={{0,1},{1,0},{2,3},{3,2},{4,5},{5,4},{6,7},{7,6},{8,9},{9,8},{10,11... | collective-permute-start | bytes 61448 | tf_op jit(solution)/shard_map/ppermute | solution.py:839

commit v4 on v3

--- a/solution.py
+++ b/solution.py
@@ -160,7 +160,7 @@
 
 
 def distances(count):
-    return [0, count - 1] + list(range(1, count - 1))
+    return [0] + list(range(count - 1, 0, -1))
 
 
 def gather_parts(parts, buf):

time: 51.4 us -> 52.3 us (1.018)
  blocking collectives: 9.41 us -> 10.2 us
  waiting for transfers between devices: 14.4 us -> 15 us
    all_to_all x1, blocking collectives: 9.41 us -> 10.2 us  [shards(): squares = lax.all_to_all(squares, ('chain', 'sub'), 0, 0, tiled=True)]
    ppermute x6, waiting for transfers between devices: 8.46 us -> 9.08 us  [exchange(): lax.ppermute(part, 'chain', [(i, i ^ x) for i in range(count)])]
    ppermute x1, waiting for transfers between devices: 2.92 us -> 2.39 us  [shards(): lax.ppermute(offer, 'chain', [p for i in range(half) for p in ((i, i + ha...]
  transfers between devices with their start and end apart: 10 -> 10, of which waited for: 9 -> 8; matrix products, arithmetic and copies ran while one was open for 0% -> 0% of each run, Pallas kernels for 3% -> 3%
where the time goes in v4:
time: 52.3 us; the launch traced here: 52.1 us
  waiting for transfers between devices  15 us (29%)
  Pallas kernels  13.4 us (26%)
  starting transfers between devices  12.9 us (25%)
  blocking collectives  10.2 us (20%)
  between operations  0.69 us (1%)
    pallas_call x7, Pallas kernels, call(): pl.pallas_call(kernel, out_shape=[jax.ShapeDtypeStruct(o[0], (o + (jnp.fl...  13.4 us
    all_to_all x1, blocking collectives, shards(): squares = lax.all_to_all(squares, ('chain', 'sub'), 0, 0, tiled=True)  10.2 us
    ppermute x6, waiting for transfers between devices, exchange(): lax.ppermute(part, 'chain', [(i, i ^ x) for i in range(count)])  9.08 us
    ppermute x6, starting transfers between devices, exchange(): lax.ppermute(part, 'chain', [(i, i ^ x) for i in range(count)])  8.25 us
    ppermute x1, waiting for transfers between devices, shards(): tail = lax.ppermute(tail, 'chain', [(i, (i + 1) % n) for i in range(n)])  3.23 us
    ppermute x1, starting transfers between devices, shards(): lax.ppermute(offer, 'chain', [p for i in range(half) for p in ((i, i + ha...  2.66 us
    ppermute x1, waiting for transfers between devices, shards(): lax.ppermute(offer, 'chain', [p for i in range(half) for p in ((i, i + ha...  2.39 us
    ppermute x2, starting transfers between devices, shards(): lax.ppermute(edge, 'sub', [p for i, j in pairs for p in ((i, j), (j, i))])  1.61 us
  transfers between devices with their start and end apart: 10, of which 8 were waited for; matrix products, arithmetic and copies ran while one was open for 0% of the time, Pallas kernels for 3%

profile of v4, /device:TPU:0, one launch (start us, length us, event | category | flops | bytes accessed | tf_op | source)
XLA Modules:
  0.0 52.1 jit_solution(6296859605977903244)
XLA Ops:
  0.6 6.0 %shard_map.95 = (f32[30,8,128]{2,1,0:T(8,128)S(1)}, f32[30,8,128]{2,1,0:T(8,128)S(1)}, f32[30,8,128]{2,1,0:T(8,128)S(1)}, f32[30,8,128]{2,1,0:T(8,128)S(1)}, f32...) custom-call(f32[24,5,8,128]{3,2,1,0:T(8,128)} %refs_0_.1, ...), custom_call_target="tpu_custom_call" | custom-call | tf_op jit(solution)/shard_map/pallas_call | solution.py:743
  6.6 4.0 %collective-permute-start = (f32[30,8,128]{2,1,0:T(8,128)S(1)}, f32[30,8,128]{2,1,0:T(8,128)S(1)}, u32[]{:S(2)}, u32[]{:S(2)}) collective-permute-start(f32[30,8,128]{2,1,0:T(8,128)S(1)} %get-tuple-element.31), channel_id=1, source_target_pairs={{0,12},{4,8},{8,4},{12,0},{16,28},{20,24},{24,20},{28,16},{1,13},{... | collective-permute-start | bytes 368648 | tf_op jit(solution)/shard_map/ppermute | solution.py:200
  10.7 0.4 collective-permute-start.1
  11.3 3.5 %collective-permute-done.refs_1_ = f32[30,8,128]{2,1,0:T(8,128)S(1)} collective-permute-done((f32[30,8,128]{2,1,0:T(8,128)S(1)}, f32[30,8,128]{2,1,0:T(8,128)S(1)}, u32[]{:S(2)}, u32[]{:S(2)}) %collective-permute-start) | collective-permute-done | bytes 122912 | tf_op jit(solution)/shard_map/ppermute | solution.py:200
  14.8 2.0 %collective-permute-done.1.refs_2_ = f32[30,8,128]{2,1,0:T(8,128)S(1)} collective-permute-done((f32[30,8,128]{2,1,0:T(8,128)S(1)}, f32[30,8,128]{2,1,0:T(8,128)S(1)}, u32[]{:S(2)}, u32[]{:S(2)}) %collective-permute-start.1) | collective-permute-done | bytes 122912 | tf_op jit(solution)/shard_map/ppermute | solution.py:200
  16.8 1.3 %shard_map.96 = (f32[2816,128]{1,0:T(8,128)S(1)}, f32[4,8,8,128]{3,2,1,0:T(8,128)S(1)}, f32[12,8,128]{2,1,0:T(8,128)S(1)}) custom-call(f32[30,8,128]{2,1,0:T(8,128)S(1)} %get-tuple-element.30.refs_0_, f32[30,8,128]{2,1,0:T(8,128)S(1)} %collective-permute-done.refs_1_, f32[30,8,128]{2,1,0:T(8,128)S(1)} %collective-permute-done.1.refs_2_, ...), custom_call_target="tpu_custom_call" | custom-call | tf_op jit(solution)/shard_map/pallas_call | solution.py:743
  18.1 2.7 %collective-permute-start.3 = (f32[12,8,128]{2,1,0:T(8,128)S(1)}, f32[12,8,128]{2,1,0:T(8,128)S(1)}, u32[]{:S(2)}, u32[]{:S(2)}) collective-permute-start(f32[12,8,128]{2,1,0:T(8,128)S(1)} %get-tuple-element.36.refs_2_), channel_id=1, source_target_pairs={{0,16},{16,0},{4,20},{20,4},{8,24},{24,8},{12,28},{28,12},{1,17},{... | collective-permute-start | bytes 147464 | tf_op jit(solution)/shard_map/ppermute | solution.py:811
  20.8 2.4 %collective-permute-done.3.refs_3_ = f32[12,8,128]{2,1,0:T(8,128)S(1)} collective-permute-done((f32[12,8,128]{2,1,0:T(8,128)S(1)}, f32[12,8,128]{2,1,0:T(8,128)S(1)}, u32[]{:S(2)}, u32[]{:S(2)}) %collective-permute-start.3) | collective-permute-done | bytes 49184 | tf_op jit(solution)/shard_map/ppermute | solution.py:811
  23.2 0.3 shard_map.97
  23.5 2.5 %collective-permute-start.4 = (f32[8,8,128]{2,1,0:T(8,128)S(1)}, f32[8,8,128]{2,1,0:T(8,128)S(1)}, u32[]{:S(2)}, u32[]{:S(2)}) collective-permute-start(f32[8,8,128]{2,1,0:T(8,128)S(1)} %get-tuple-element.38), channel_id=1, source_target_pairs={{0,12},{4,8},{8,4},{12,0},{16,28},{20,24},{24,20},{28,16},{1,13},{... | collective-permute-start | bytes 98312 | tf_op jit(solution)/shard_map/ppermute | solution.py:200
  26.0 0.7 %collective-permute-start.5 = (f32[8,8,128]{2,1,0:T(8,128)S(1)}, f32[8,8,128]{2,1,0:T(8,128)S(1)}, u32[]{:S(2)}, u32[]{:S(2)}) collective-permute-start(f32[8,8,128]{2,1,0:T(8,128)S(1)} %get-tuple-element.39), channel_id=1, source_target_pairs={{0,8},{4,12},{8,0},{12,4},{16,24},{20,28},{24,16},{28,20},{1,9},{5... | collective-permute-start | bytes 98312 | tf_op jit(solution)/shard_map/ppermute | solution.py:200
  26.7 0.3 collective-permute-start.6
  27.0 1.3 %collective-permute-done.4.refs_1_ = f32[8,8,128]{2,1,0:T(8,128)S(1)} collective-permute-done((f32[8,8,128]{2,1,0:T(8,128)S(1)}, f32[8,8,128]{2,1,0:T(8,128)S(1)}, u32[]{:S(2)}, u32[]{:S(2)}) %collective-permute-start.4) | collective-permute-done | bytes 32800 | tf_op jit(solution)/shard_map/ppermute | solution.py:200
  28.3 1.6 %collective-permute-done.5.refs_2_ = f32[8,8,128]{2,1,0:T(8,128)S(1)} collective-permute-done((f32[8,8,128]{2,1,0:T(8,128)S(1)}, f32[8,8,128]{2,1,0:T(8,128)S(1)}, u32[]{:S(2)}, u32[]{:S(2)}) %collective-permute-start.5) | collective-permute-done | bytes 32800 | tf_op jit(solution)/shard_map/ppermute | solution.py:200
  29.9 0.7 %collective-permute-done.6.refs_3_ = f32[8,8,128]{2,1,0:T(8,128)S(1)} collective-permute-done((f32[8,8,128]{2,1,0:T(8,128)S(1)}, f32[8,8,128]{2,1,0:T(8,128)S(1)}, u32[]{:S(2)}, u32[]{:S(2)}) %collective-permute-start.6) | collective-permute-done | bytes 32800 | tf_op jit(solution)/shard_map/ppermute | solution.py:200
  30.6 2.2 %shard_map.98 = (f32[24,5,8,128]{3,2,1,0:T(8,128)S(1)}, f32[25,5,8,128]{3,2,1,0:T(8,128)S(1)}, f32[3,5,8,128]{3,2,1,0:T(8,128)S(1)}, f32[5,8,128]{2,1,0:T(8,128)...) custom-call(f32[8,8,128]{2,1,0:T(8,128)S(1)} %get-tuple-element.37.refs_0_, ...), custom_call_target="tpu_custom_call" | custom-call | tf_op jit(solution)/shard_map/pallas_call | solution.py:743
  32.8 0.4 collective-permute-start.7
  33.2 1.6 %collective-permute-start.8 = (f32[5,8,128]{2,1,0:T(8,128)S(1)}, f32[5,8,128]{2,1,0:T(8,128)S(1)}, u32[]{:S(2)}, u32[]{:S(2)}) collective-permute-start(f32[5,8,128]{2,1,0:T(8,128)S(1)} %get-tuple-element.55), channel_id=1, source_target_pairs={{0,1},{1,0},{2,3},{3,2},{4,5},{5,4},{6,7},{7,6},{8,9},{9,8},{10,11... | collective-permute-start | bytes 61448 | tf_op jit(solution)/shard_map/ppermute | solution.py:839
  34.8 1.5 %shard_map.99 = (f32[24,5,8,128]{3,2,1,0:T(8,128)S(1)}, f32[7,8,128]{2,1,0:T(8,128)S(1)}, f32[24,5,8,128]{3,2,1,0:T(8,128)}) custom-call(f32[24,5,8,128]{3,2,1,0:T(8,128)S(1)} %get-tuple-element.47.z, f32[25,5,8,128]{3,2,1,0:T(8,128)S(1)} %get-tuple-element.48.w, f32[1250,128]{1,0:T(8,128)S(1)} %get-tuple-element.49.low, ...), custom_call_target="tpu_custom_call" | custom-call | tf_op jit(solution)/shard_map/pallas_call | solution.py:743
  36.3 0.3 collective-permute-done.9.swap_b
  36.6 3.2 %collective-permute-done.7.tail = f32[3,5,8,128]{3,2,1,0:T(8,128)S(1)} collective-permute-done((f32[3,5,8,128]{3,2,1,0:T(8,128)S(1)}, f32[3,5,8,128]{3,2,1,0:T(8,128)S(1)}, u32[]{:S(2)}, u32[]{:S(2)}) %collective-permute-start.7) | collective-permute-done | bytes 61472 | tf_op jit(solution)/shard_map/ppermute | solution.py:837
  39.8 1.1 %shard_map.100 = (f32[24,5,8,128]{3,2,1,0:T(8,128)S(1)}, f32[32,1,128]{2,1,0:T(1,128)S(1)}) custom-call(f32[24,5,8,128]{3,2,1,0:T(8,128)S(1)} %get-tuple-element.52.inner, f32[7,8,128]{2,1,0:T(8,128)S(1)} %get-tuple-element.53.coef, f32[1250,128]{1,0:T(8,128)S(1)} %get-tuple-element.49.low, f32[3,5,8,128]{3,2,1,0:T(8,128)S(1)} %collective-permute-done.7.tail, ...), custom_call_target="tpu_custom_call" | custom-call | tf_op jit(solution)/shard_map/pallas_call | solution.py:743
  41.0 10.2 %all_to_all.5.squares = f32[32,1,128]{2,1,0:T(1,128)S(1)} all-to-all(f32[32,1,128]{2,1,0:T(1,128)S(1)} %get-tuple-element.57), channel_id=1, replica_groups=mesh['chain'=8,'sub'=4] {'chain','sub'}, dimensions={0} | all-to-all | bytes 32768 | tf_op jit(solution)/shard_map/all_to_all | solution.py:863
  51.2 0.9 %shard_map.101 = f32[24,5,8,128]{3,2,1,0:T(8,128)} custom-call(f32[24,5,8,128]{3,2,1,0:T(8,128)S(1)} %get-tuple-element.56.resid, f32[32,1,128]{2,1,0:T(1,128)S(1)} %all_to_all.5.squares), custom_call_target="tpu_custom_call" | custom-call | tf_op jit(solution)/shard_map/pallas_call | solution.py:743
  (4 shorter events, 0.2 us)
Async XLA Ops:
  6.6 8.2 %collective-permute-start = (f32[30,8,128]{2,1,0:T(8,128)S(1)}, f32[30,8,128]{2,1,0:T(8,128)S(1)}, u32[]{:S(2)}, u32[]{:S(2)}) collective-permute-start(f32[30,8,128]{2,1,0:T(8,128)S(1)} %get-tuple-element.31), channel_id=1, source_target_pairs={{0,12},{4,8},{8,4},{12,0},{16,28},{20,24},{24,20},{28,16},{1,13},{... | collective-permute-start | bytes 368648 | tf_op jit(solution)/shard_map/ppermute | solution.py:200
  10.7 6.1 %collective-permute-start.1 = (f32[30,8,128]{2,1,0:T(8,128)S(1)}, f32[30,8,128]{2,1,0:T(8,128)S(1)}, u32[]{:S(2)}, u32[]{:S(2)}) collective-permute-start(f32[30,8,128]{2,1,0:T(8,128)S(1)} %get-tuple-element.32), channel_id=1, source_target_pairs={{0,8},{4,12},{8,0},{12,4},{16,24},{20,28},{24,16},{28,20},{1,9},{5... | collective-permute-start | bytes 368648 | tf_op jit(solution)/shard_map/ppermute | solution.py:200
  11.1 5.7 %collective-permute-start.2 = (f32[30,8,128]{2,1,0:T(8,128)S(1)}, f32[30,8,128]{2,1,0:T(8,128)S(1)}, u32[]{:S(2)}, u32[]{:S(2)}) collective-permute-start(f32[30,8,128]{2,1,0:T(8,128)S(1)} %get-tuple-element.33), channel_id=1, source_target_pairs={{0,4},{4,0},{8,12},{12,8},{16,20},{20,16},{24,28},{28,24},{1,5},{5... | collective-permute-start | bytes 368648 | tf_op jit(solution)/shard_map/ppermute | solution.py:200
  18.1 5.1 %collective-permute-start.3 = (f32[12,8,128]{2,1,0:T(8,128)S(1)}, f32[12,8,128]{2,1,0:T(8,128)S(1)}, u32[]{:S(2)}, u32[]{:S(2)}) collective-permute-start(f32[12,8,128]{2,1,0:T(8,128)S(1)} %get-tuple-element.36.refs_2_), channel_id=1, source_target_pairs={{0,16},{16,0},{4,20},{20,4},{8,24},{24,8},{12,28},{28,12},{1,17},{... | collective-permute-start | bytes 147464 | tf_op jit(solution)/shard_map/ppermute | solution.py:811
  23.5 4.9 %collective-permute-start.4 = (f32[8,8,128]{2,1,0:T(8,128)S(1)}, f32[8,8,128]{2,1,0:T(8,128)S(1)}, u32[]{:S(2)}, u32[]{:S(2)}) collective-permute-start(f32[8,8,128]{2,1,0:T(8,128)S(1)} %get-tuple-element.38), channel_id=1, source_target_pairs={{0,12},{4,8},{8,4},{12,0},{16,28},{20,24},{24,20},{28,16},{1,13},{... | collective-permute-start | bytes 98312 | tf_op jit(solution)/shard_map/ppermute | solution.py:200
  26.0 3.9 %collective-permute-start.5 = (f32[8,8,128]{2,1,0:T(8,128)S(1)}, f32[8,8,128]{2,1,0:T(8,128)S(1)}, u32[]{:S(2)}, u32[]{:S(2)}) collective-permute-start(f32[8,8,128]{2,1,0:T(8,128)S(1)} %get-tuple-element.39), channel_id=1, source_target_pairs={{0,8},{4,12},{8,0},{12,4},{16,24},{20,28},{24,16},{28,20},{1,9},{5... | collective-permute-start | bytes 98312 | tf_op jit(solution)/shard_map/ppermute | solution.py:200
  26.7 3.9 %collective-permute-start.6 = (f32[8,8,128]{2,1,0:T(8,128)S(1)}, f32[8,8,128]{2,1,0:T(8,128)S(1)}, u32[]{:S(2)}, u32[]{:S(2)}) collective-permute-start(f32[8,8,128]{2,1,0:T(8,128)S(1)} %get-tuple-element.40), channel_id=1, source_target_pairs={{0,4},{4,0},{8,12},{12,8},{16,20},{20,16},{24,28},{28,24},{1,5},{5... | collective-permute-start | bytes 98312 | tf_op jit(solution)/shard_map/ppermute | solution.py:200
  32.8 7.0 %collective-permute-start.7 = (f32[3,5,8,128]{3,2,1,0:T(8,128)S(1)}, f32[3,5,8,128]{3,2,1,0:T(8,128)S(1)}, u32[]{:S(2)}, u32[]{:S(2)}) collective-permute-start(f32[3,5,8,128]{3,2,1,0:T(8,128)S(1)} %get-tuple-element.54), channel_id=1, source_target_pairs={{0,4},{4,8},{8,12},{12,16},{16,20},{20,24},{24,28},{28,0},{1,5},{5... | collective-permute-start | bytes 184328 | tf_op jit(solution)/shard_map/ppermute | solution.py:837
  33.2 3.4 %collective-permute-start.9 = (f32[5,8,128]{2,1,0:T(8,128)S(1)}, f32[5,8,128]{2,1,0:T(8,128)S(1)}, u32[]{:S(2)}, u32[]{:S(2)}) collective-permute-start(f32[5,8,128]{2,1,0:T(8,128)S(1)} %get-tuple-element.55), channel_id=1, source_target_pairs={{1,2},{2,1},{0,3},{3,0},{5,6},{6,5},{4,7},{7,4},{9,10},{10,9},{8,1... | collective-permute-start | bytes 61448 | tf_op jit(solution)/shard_map/ppermute | solution.py:839
  33.2 3.4 %collective-permute-start.8 = (f32[5,8,128]{2,1,0:T(8,128)S(1)}, f32[5,8,128]{2,1,0:T(8,128)S(1)}, u32[]{:S(2)}, u32[]{:S(2)}) collective-permute-start(f32[5,8,128]{2,1,0:T(8,128)S(1)} %get-tuple-element.55), channel_id=1, source_target_pairs={{0,1},{1,0},{2,3},{3,2},{4,5},{5,4},{6,7},{7,6},{8,9},{9,8},{10,11... | collective-permute-start | bytes 61448 | tf_op jit(solution)/shard_map/ppermute | solution.py:839
